TPU v7x, 32 devices: a whole 2x2x4 slice. The times are simulated.
32 devices in a mesh: pool: 2 (over y), dp: 8 (over z, x), tensor: 2 (over core).
Axes of the slice: x: 2, y: 2, z: 4, core: 2. Of those that a mesh axis runs over, the one named last changes fastest.
Arguments:
- train_out: bfloat16 [2048, 4096], P(('pool', 'dp'), 'tensor'), parts along dimension 0, may hold values from -3 to 3
- train_in: bfloat16 [2048, 14336], P(('pool', 'dp'), 'tensor'), parts along dimension 0, may hold values from -6 to 6
- query_out: bfloat16 [128, 4096], P(None, 'dp'), may hold values from -0.08984375 to 0.08984375
- query_in: bfloat16 [128, 14336], P('dp', 'tensor'), may hold values from -0.044921875 to 0.044921875
- basis_out: bfloat16 [4096, 4096], P('dp', 'tensor'), may hold values from -0.09375 to 0.09375
- basis_in: bfloat16 [14336, 14336], P('tensor', 'dp'), may hold values from -0.046875 to 0.046875
- eigval: bfloat16 [4096, 14336], P('tensor', 'dp'), may hold values from 0.049804688 to 5
- sketch_bucket: int32 [14336], P('dp'), may hold values from 0 to 7
- sketch_sign: int32 [14336], P('dp'), may hold values from 0 to 1
- lengths: int32 [16, 4], P(('pool', 'dp')), parts along dimension 0, may hold values from 1 to 64, 128 in all within a row
- source_of_seq: int32 [64], P(('pool', 'dp')), parts along dimension 0, may hold values from 0 to 31
Outputs:
- scores: float32 [64, 8], P(('pool', 'dp')), parts along dimension 0
- source_totals: float32 [64, 8], P('pool'), parts along dimension 0
There are 2 independent parts, one for each index of `pool`. A program takes and returns all parts, laid end to end along the dimension named above; an argument that names none is the same for every part. Nothing has to cross between parts.
Inputs may be any that keep to these rules, and one draw needn't show every extreme that they name: `lengths`: row j holds the token counts of the 4 sequences of dp index j in order; each row sums to 128 and its largest count is half of 128.
All inputs are finite; a program needn't handle non-finite values.
Results may differ from a plain program's by a relative error of at most 0.0003.
Values may be sent and summed in bfloat16 or wider, within the bound.
A program may use at most 320 MiB of HBM per device.

v0:
```python
import jax
import jax.numpy as jnp
from jax import lax
from jax.sharding import PartitionSpec as P

QUERIES = 8
QLEN = 16
RANK = 8
SOURCES = 32


DAMP = 0.1


def sketch_table(bucket_ids, sign_bits):
    column_ids = jnp.arange(RANK, dtype=jnp.int32)
    signs = (2 * sign_bits - 1).astype(jnp.float32)
    return jnp.where(bucket_ids[:, None] == column_ids[None, :], signs[:, None], jnp.float32(0.0))


def seq_totals(proj_out, proj_in, seq_starts, seq_ends):
    token_score = (proj_out * proj_in).reshape(proj_out.shape[0], QUERIES, RANK).sum(axis=2)
    positions = jnp.arange(proj_out.shape[0], dtype=jnp.int32)
    member = (
        (positions[None, :] >= seq_starts[:, None]) & (positions[None, :] < seq_ends[:, None])
    ).astype(jnp.float32)
    return jnp.dot(member, token_score, precision=lax.Precision.HIGHEST)


def body(
    train_out,
    train_in,
    query_out,
    query_in,
    basis_out,
    basis_in,
    eigval,
    sketch_bucket,
    sketch_sign,
    lengths,
    source_of_seq,
):
    factor_cols = QUERIES * RANK
    half_rows = basis_out.shape[1]
    own_cols = basis_in.shape[1]
    in_part = jnp.dot(
        lax.all_gather(query_in, "dp", axis=0, tiled=True),
        basis_in,
        preferred_element_type=jnp.float32,
    )
    out_part = lax.dot_general(
        basis_out, query_out, (((0,), (1,)), ((), ())), preferred_element_type=jnp.float32
    )
    rotated_out = lax.psum(out_part, "dp")
    rotated_in = lax.psum(in_part, "tensor")
    out_blocks = rotated_out.reshape(half_rows, QUERIES, QLEN)
    in_blocks = rotated_in.reshape(QUERIES, QLEN, own_cols)
    eig_plus = eigval.astype(jnp.float32) + DAMP
    precond = (
        jnp.einsum("eqi,qif->qef", out_blocks, in_blocks, precision=lax.Precision.HIGHEST)
        / eig_plus[None]
    )
    sketch = sketch_table(sketch_bucket, sketch_sign)
    sketch_part = jnp.einsum(
        "qef,fk->eqk", precond, sketch, precision=lax.Precision.HIGHEST
    ).reshape(half_rows, factor_cols)
    sketched = lax.psum(sketch_part, "dp").reshape(half_rows, QUERIES, RANK)
    gram_part = jnp.einsum("eqk,eql->qkl", sketched, sketched, precision=lax.Precision.HIGHEST)
    gram_matrix = lax.psum(gram_part, "tensor")
    chol_factor = jnp.linalg.cholesky(gram_matrix)
    left_trans = jax.scipy.linalg.solve_triangular(
        chol_factor, jnp.transpose(sketched, (1, 2, 0)), lower=True
    )
    right_part = jnp.einsum(
        "qef,qke->fqk", precond, left_trans, precision=lax.Precision.HIGHEST
    ).reshape(own_cols, factor_cols)
    left_eig = jnp.transpose(left_trans, (2, 0, 1)).reshape(half_rows, factor_cols)
    basis_out_wide = basis_out.astype(jnp.float32)
    left_part = jnp.dot(basis_out_wide, left_eig, precision=lax.Precision.HIGHEST)
    right_eig, left_mine = lax.psum((right_part, left_part), "tensor")
    basis_in_wide = basis_in.astype(jnp.float32)
    right_term = jnp.dot(basis_in_wide, right_eig, precision=lax.Precision.HIGHEST)
    right_full = lax.psum(right_term, "dp")
    left_full = lax.all_gather(left_mine, "dp", axis=0, tiled=True)
    core_index = lax.axis_index("tensor")
    left_half = lax.dynamic_slice_in_dim(left_full, core_index * half_rows, half_rows, 0)
    proj_out = jnp.dot(train_out.astype(jnp.float32), left_half, precision=lax.Precision.HIGHEST)
    proj_in = jnp.dot(train_in.astype(jnp.float32), right_full, precision=lax.Precision.HIGHEST)
    seq_len = lengths[0]
    seq_ends = jnp.cumsum(seq_len)
    seq_starts = seq_ends - seq_len
    out_whole, in_whole = lax.psum((proj_out, proj_in), "tensor")
    seq_sum = seq_totals(out_whole, in_whole, seq_starts, seq_ends)
    scores = seq_sum / seq_len.astype(jnp.float32)[:, None]
    owner_table = (source_of_seq[None, :] == jnp.arange(SOURCES, dtype=jnp.int32)[:, None]).astype(
        jnp.float32
    )
    source_part = jnp.dot(owner_table, scores, precision=lax.Precision.HIGHEST)
    source_totals = lax.psum(source_part, "dp")
    return (scores, source_totals)


def solution(mesh):
    return jax.shard_map(
        body,
        mesh=mesh,
        in_specs=(
            P(("pool", "dp"), "tensor"),
            P(("pool", "dp"), "tensor"),
            P(None, "dp"),
            P("dp", "tensor"),
            P("dp", "tensor"),
            P("tensor", "dp"),
            P("tensor", "dp"),
            P("dp"),
            P("dp"),
            P(("pool", "dp"), None),
            P(("pool", "dp")),
        ),
        out_specs=(P(("pool", "dp"), None), P("pool", None)),
        check_vma=False,
    )
```

profile of v0, /device:TPU:0, one launch (start us, length us, event | category | flops | bytes accessed | tf_op | source)
XLA Modules:
  0.0 761.2 jit_solution(1983753415554233732)
XLA Ops:
  8.8 2.3 fusion.26
  11.9 47.3 %all-gather.3.cloned.1.call-done = bf16[128,7168]{1,0:T(8,128)(2,1)} async-done(((bf16[16,7168]{1,0:T(8,128)(2,1)}), bf16[128,7168]{1,0:T(8,128)(2,1)}) %all-gather.3.cloned.1.call-update) | async-done | bytes 1835024 | tf_op jit(solution)/shard_map/all_gather | solution.py:47
  59.2 13.5 %fusion.23 = f32[128,1792]{1,0:T(8,128)} fusion(bf16[128,7168]{1,0:T(8,128)(2,1)} %all-gather.3.cloned.1.call-done, bf16[7168,1792]{1,0:T(8,128)(2,1)} %param.16), kind=kOutput, calls=%fused_computation.43 | convolution fusion | flops 3288334336 | bytes 28442624 | tf_op jit(solution)/shard_map/dot_general | solution.py:46
  72.8 9.6 %convert_add_fusion = f32[2048,1792]{1,0:T(8,128)} fusion(bf16[2048,1792]{1,0:T(8,128)(2,1)} %param.17), kind=kLoop, calls=%fused_computation.3 | loop fusion | flops 7340032 | bytes 22020096 | tf_op jit(solution)/shard_map/add | solution.py:58
  82.4 57.3 %all-reduce.9.cloned.1.call-done = f32[2048,8,16]{0,2,1:T(8,128)} async-done(((f32[2048,8,16]{0,2,1:T(8,128)}), f32[2048,8,16]{0,2,1:T(8,128)}) %all-reduce.9.cloned.1.call-update) | async-done | bytes 1048592 | tf_op jit(solution)/shard_map/psum | solution.py:54
  139.7 21.5 %all-reduce.11.cloned.1.call-done = f32[8,16,1792]{2,1,0:T(8,128)} async-done(((f32[8,16,1792]{2,1,0:T(8,128)}), f32[8,16,1792]{2,1,0:T(8,128)}) %all-reduce.11.cloned.1.call-update) | async-done | bytes 917520 | tf_op jit(solution)/shard_map/psum | solution.py:55
  161.2 99.1 %fusion.24 = f32[8,2048,1792]{2,1,0:T(8,128)} fusion(f32[2048,8,16]{0,2,1:T(8,128)} %all-reduce.9.cloned.1.call-done, f32[8,16,1792]{2,1,0:T(8,128)} %all-reduce.11.cloned.1.call-done), kind=kOutput, calls=%fused_computation.44 | convolution fusion | flops 5637144576 | bytes 119406592 | tf_op jit(solution)/shard_map/eqi,qif->qef/dot_general | solution.py:60
  260.4 103.6 %fusion.2 = f32[2048,8,8]{0,2,1:T(8,128)} fusion(f32[8,2048,1792]{2,1,0:T(8,128)} %fusion.24, f32[2048,1792]{1,0:T(8,128)} %convert_add_fusion, f32[1792]{0:T(1024)S(1)} %add_convert_fusion, s32[1792]{0:T(1024)S(1)} %copy-done.4), kind=kOutput, calls=%fused_computation.5 | convolution fusion | flops 2847961088 | bytes 132659200 | tf_op jit(solution)/shard_map/qef,fk->eqk/dot_general | solution.py:64
  364.0 73.6 %all-reduce.13.cloned.1.call-done = f32[2048,8,8]{0,2,1:T(8,128)} async-done(((f32[2048,8,8]{0,2,1:T(8,128)}), f32[2048,8,8]{0,2,1:T(8,128)}) %all-reduce.13.cloned.1.call-update) | async-done | bytes 524304 | tf_op jit(solution)/shard_map/psum | solution.py:67
  437.6 2.3 fusion.25
  440.0 3.4 psum.73
  443.5 6.1 custom-call.8
  449.8 5.0 custom-call.9
  454.8 1.7 fusion.5
  456.6 65.9 %fusion.3 = f32[1792,64]{0,1:T(8,128)} fusion(f32[8,8,2048]{2,1,0:T(8,128)S(1)} %fusion.5, f32[8,2048,1792]{2,1,0:T(8,128)} %fusion.24, f32[2048,1792]{1,0:T(8,128)} %convert_add_fusion), kind=kOutput, calls=%fused_computation.6 | convolution fusion | flops 2847932416 | bytes 133103616 | tf_op jit(solution)/shard_map/qef,qke->fqk/dot_general | solution.py:74
  522.4 2.7 convolution_bitcast_fusion.1
  525.2 18.3 %all-reduce.19.cloned.1.call-done = (f32[512,64]{0,1:T(8,128)}, f32[1792,64]{0,1:T(8,128)}) async-done(((f32[512,64]{0,1:T(8,128)}, f32[1792,64]{0,1:T(8,128)}), (f32[512,64]{0,1:T(8,128)}, f32[1792,64]{0,1:T(8,128)})) %all-reduce.19.cloned.1.call-update) | async-done | bytes 589840 | tf_op jit(solution)/shard_map/psum | solution.py:80
  543.5 28.9 %convolution_bitcast_fusion = f32[7168,64]{0,1:T(8,128)} fusion(f32[1792,64]{0,1:T(8,128)} %get-tuple-element.5, bf16[7168,1792]{1,0:T(8,128)(2,1)} %param.16), kind=kOutput, calls=%fused_computation.4 | convolution fusion | flops 9865003008 | bytes 27983872 | tf_op jit(solution)/shard_map/dot_general | solution.py:82
  573.4 96.0 %all-reduce.15.cloned.1.call-done = f32[7168,64]{0,1:T(8,128)} async-done(((f32[7168,64]{0,1:T(8,128)}), f32[7168,64]{0,1:T(8,128)}) %all-reduce.15.cloned.1.call-update) | async-done | bytes 1835024 | tf_op jit(solution)/shard_map/psum | solution.py:83
  669.5 4.7 convolution_bitcast_fusion.2
  674.2 37.4 %all-gather.5.cloned.1.call-done = f32[4096,64]{0,1:T(8,128)} async-done(((f32[512,64]{0,1:T(8,128)}), f32[4096,64]{0,1:T(8,128)}) %all-gather.5.cloned.1.call-update) | async-done | bytes 1048592 | tf_op jit(solution)/shard_map/all_gather | solution.py:84
  711.5 2.3 convolution_bitcast_fusion.3
  713.9 16.7 %all-reduce.17.cloned.1.call-done = (f32[128,64]{0,1:T(8,128)}, f32[128,64]{0,1:T(8,128)}) async-done(((f32[128,64]{0,1:T(8,128)}, f32[128,64]{0,1:T(8,128)}), (f32[128,64]{0,1:T(8,128)}, f32[128,64]{0,1:T(8,128)})) %all-reduce.17.cloned.1.call-update) | async-done | bytes 65552 | tf_op jit(solution)/shard_map/psum | solution.py:92
  731.7 22.2 %psum.79 = f32[32,8]{0,1:T(8,128)} all-reduce(f32[32,8]{0,1:T(8,128)S(1)} %fusion.15), channel_id=1, replica_groups=mesh['pool'=2,'dp'=8,'tensor'=2] {'dp'}, use_global_device_ids=true, to_apply=%region_13.14 | all-reduce | flops 256 | bytes 2048 | tf_op jit(solution)/shard_map/psum | solution.py:99
  (42 shorter events, 5.0 us)
Async XLA Ops:
  7.2 1.6 copy-start
  7.2 52.0 %all-gather.3.cloned.1.call-start = ((), (), s32[]{:S(2)}) async-start(), calls=%async_computation.1 | async-start | bytes 2064384 | tf_op jit(solution)/shard_map/all_gather | solution.py:47
  7.9 131.8 %all-reduce.9.cloned.1.call-start = ((), (), s32[]{:S(2)}) async-start(), calls=%async_computation | async-start | bytes 2097152 | tf_op jit(solution)/shard_map/psum | solution.py:54
  11.1 150.1 %all-reduce.11.cloned.1.call-start = ((), (), s32[]{:S(2)}) async-start(), calls=%async_computation.2 | async-start | bytes 1835008 | tf_op jit(solution)/shard_map/psum | solution.py:55
  72.7 364.9 %all-reduce.13.cloned.1.call-start = ((), (), s32[]{:S(2)}) async-start(), calls=%async_computation.3 | async-start | bytes 1048576 | tf_op jit(solution)/shard_map/psum | solution.py:67
  82.4 178.0 %copy-start.4 = (s32[1792]{0:T(1024)S(1)}, s32[1792]{0:T(1024)}, u32[]{:S(2)}) copy-start(s32[1792]{0:T(1024)} %param.18) | copy-start | bytes 21508
  364.0 179.5 %all-reduce.19.cloned.1.call-start = ((), (), s32[]{:S(2)}) async-start(), calls=%async_computation.7 | async-start | bytes 1179648 | tf_op jit(solution)/shard_map/psum | solution.py:80
  525.1 144.4 %all-reduce.15.cloned.1.call-start = ((), (), s32[]{:S(2)}) async-start(), calls=%async_computation.5 | async-start | bytes 3670016 | tf_op jit(solution)/shard_map/psum | solution.py:83
  543.5 29.8 %copy-start.5 = (s32[1,4]{1,0:T(1,128)S(1)}, s32[1,4]{1,0:T(1,128)}, u32[]{:S(2)}) copy-start(s32[1,4]{1,0:T(1,128)} %param.20) | copy-start | bytes 52
  543.5 168.1 %copy-start.1 = (bf16[128,2048]{1,0:T(8,128)(2,1)S(1)}, bf16[128,2048]{1,0:T(8,128)(2,1)}, u32[]{:S(2)}) copy-start(bf16[128,2048]{1,0:T(8,128)(2,1)} %param.11) | copy-start | bytes 1572868
  543.5 188.0 %copy-start.3 = (s32[4]{0:T(128)S(1)}, s32[4]{0:T(128)}, u32[]{:S(2)}) copy-start(s32[4]{0:T(128)} %param.21) | copy-start | bytes 52
  572.4 139.1 %all-gather.5.cloned.1.call-start = ((), (), s32[]{:S(2)}) async-start(), calls=%async_computation.4 | async-start | bytes 1179648 | tf_op jit(solution)/shard_map/all_gather | solution.py:84
  573.2 157.3 %all-reduce.17.cloned.1.call-start = ((), (), s32[]{:S(2)}) async-start(), calls=%async_computation.6 | async-start | bytes 131072 | tf_op jit(solution)/shard_map/psum | solution.py:92
  731.5 22.4 %copy-start.2 = (f32[4,8]{1,0:T(4,128)}, f32[4,8]{1,0:T(4,128)S(1)}, u32[]{:S(2)}) copy-start(f32[4,8]{1,0:T(4,128)S(1)} %convolution_divide_fusion) | copy-start | bytes 388
Sparse Core Ops, SparseCore 0:
  10.2 48.9 all-gather.2
  62.7 77.0 all-reduce.8
  142.2 18.9 all-reduce.10
  364.1 73.5 all-reduce.12
  525.2 18.1 all-reduce.18
  572.6 96.8 all-reduce.14
  671.7 39.8 all-gather.4
  714.0 16.5 all-reduce.16
where the time goes:
time: 766 us; the launch traced here: 761 us
  waiting for transfers between devices  370 us (48%)
  matrix products  327 us (43%)
  blocking collectives  25.6 us (3%)
  other arithmetic  22.7 us (3%)
  between operations  14.7 us (2%)
    dot_general x1, matrix products, body(): jnp.einsum('qef,fk->eqk', precond, sketch, precision=lax.Precision.HIGHEST)  104 us
    dot_general x1, matrix products, body(): jnp.einsum('eqi,qif->qef', out_blocks, in_blocks, precision=lax.Precision...  99.1 us
    psum x1, waiting for transfers between devices, body(): right_full = lax.psum(right_term, 'dp')  96 us
    psum x1, waiting for transfers between devices, body(): sketched = lax.psum(sketch_part, 'dp').reshape(half_rows, QUERIES, RANK)  73.6 us
    dot_general x1, matrix products, body(): jnp.einsum('qef,qke->fqk', precond, left_trans, precision=lax.Precision.H...  65.9 us
    psum x1, waiting for transfers between devices, body(): rotated_out = lax.psum(out_part, 'dp')  57.3 us
    all_gather x1, waiting for transfers between devices, body(): lax.all_gather(query_in, 'dp', axis=0, tiled=True)  47.3 us
    all_gather x1, waiting for transfers between devices, body(): left_full = lax.all_gather(left_mine, 'dp', axis=0, tiled=True)  37.4 us
  transfers between devices with their start and end apart: 8, of which 8 were waited for; matrix products, arithmetic and copies ran while one was open for 4% of the time, Pallas kernels for 0%

commit v1 on v0

--- a/solution.py
+++ b/solution.py
@@ -1,6 +1,10 @@
+import functools
+
 import jax
 import jax.numpy as jnp
 from jax import lax
+from jax.experimental import pallas as pl
+from jax.experimental.pallas import tpu as pltpu
 from jax.sharding import PartitionSpec as P
 
 QUERIES = 8
@@ -10,6 +14,553 @@
 
 
 DAMP = 0.1
+
+F32 = jnp.float32
+BF16 = jnp.bfloat16
+MESH = pl.DeviceIdType.MESH
+NT = (((1,), (1,)), ((), ()))
+NN = (((1,), (0,)), ((), ()))
+HALF_Q = QUERIES // 2
+HALF_TOK = HALF_Q * QLEN
+HALF_COLS = HALF_Q * RANK
+VMEM = pl.BlockSpec(memory_space=pltpu.VMEM)
+
+
+def split(x):
+    hi = x.astype(BF16)
+    return hi, (x - hi.astype(F32)).astype(BF16)
+
+
+def mm(a, b, dims):
+    return lax.dot_general(a, b, dims, preferred_element_type=F32)
+
+
+def greet(targets):
+    barrier = pltpu.get_barrier_semaphore()
+    for target in targets:
+        pl.semaphore_signal(barrier, inc=1, device_id=target, device_id_type=MESH)
+    pl.semaphore_wait(barrier, len(targets))
+
+
+def remote(src, dst, send, recv, target):
+    return pltpu.make_async_remote_copy(
+        src_ref=src, dst_ref=dst, send_sem=send, recv_sem=recv,
+        device_id=target, device_id_type=MESH,
+    )
+
+
+def params(collective_id):
+    return pltpu.CompilerParams(
+        collective_id=collective_id, has_side_effects=True, vmem_limit_bytes=56 << 20
+    )
+
+
+def gather_kernel(n, qin, part, q_all, a_out, recv, q_send, q_recv, rs_send, rs_recv, ag_send, ag_recv):
+    d = lax.axis_index("dp")
+    p = lax.axis_index("pool")
+    rows = part.shape[0] // n
+    peers = [lax.rem(d + k, n) for k in range(n)]
+    greet([{"dp": peers[k]} for k in range(1, n)])
+
+    def scatter(k):
+        return remote(
+            part.at[pl.ds(pl.multiple_of(peers[k] * rows, rows), rows)], recv.at[k],
+            rs_send.at[k], rs_recv.at[k], {"dp": peers[k]},
+        )
+
+    for k in range(1, n):
+        scatter(k).start()
+    mine = d // 2
+    is_sender = d == 2 * mine + lax.rem(mine + p, 2)
+
+    def query_copy(j, k):
+        return remote(
+            qin, q_all.at[pl.ds(pl.multiple_of(j * QLEN, QLEN), QLEN)],
+            q_send.at[k], q_recv.at[j], {"dp": peers[k]},
+        )
+
+    @pl.when(is_sender)
+    def _():
+        for k in range(1, n):
+            query_copy(mine, k).start()
+        q_all[pl.ds(pl.multiple_of(mine * QLEN, QLEN), QLEN), :] = qin[...]
+
+    for k in range(1, n):
+        scatter(k).wait_recv()
+    own = pl.ds(pl.multiple_of(d * rows, rows), rows)
+    total = part[own, :]
+    for k in range(1, n):
+        total = total + recv[k]
+    a_out[own, :] = total
+
+    def share(k):
+        return remote(a_out.at[own], a_out.at[own], ag_send.at[k], ag_recv.at[k], {"dp": peers[k]})
+
+    for k in range(1, n):
+        share(k).start()
+    for k in range(1, n):
+        source = lax.rem(d + n - k, n)
+        theirs = pl.ds(pl.multiple_of(source * rows, rows), rows)
+        remote(a_out.at[own], a_out.at[theirs], ag_send.at[k], ag_recv.at[k], {"dp": peers[k]}).wait_recv()
+        scatter(k).wait_send()
+        share(k).wait_send()
+    for j in range(HALF_Q):
+        @pl.when(d != 2 * j + lax.rem(j + p, 2))
+        def _():
+            query_copy(j, 1).wait_recv()
+
+    @pl.when(is_sender)
+    def _():
+        for k in range(1, n):
+            query_copy(mine, k).wait_send()
+
+
+def gather(n, query_in, out_part):
+    dma = pltpu.SemaphoreType.DMA
+    return pl.pallas_call(
+        functools.partial(gather_kernel, n),
+        out_shape=(
+            jax.ShapeDtypeStruct((HALF_TOK, query_in.shape[1]), BF16),
+            jax.ShapeDtypeStruct(out_part.shape, F32),
+        ),
+        in_specs=[VMEM] * 2,
+        out_specs=(VMEM, VMEM),
+        scratch_shapes=[
+            pltpu.VMEM((n, out_part.shape[0] // n, out_part.shape[1]), F32),
+            dma((n,)), dma((HALF_Q,)), dma((n,)), dma((n,)), dma((n,)), dma((n,)),
+        ],
+        compiler_params=params(0),
+    )(query_in, out_part)
+
+
+def rotate_kernel(tiles, q_all, basis, out, part, recv, send_sem, recv_sem):
+    i = pl.program_id(0)
+    partner = {"tensor": 1 - lax.axis_index("tensor")}
+
+    @pl.when(i == 0)
+    def _():
+        greet([partner])
+
+    part[i] = mm(q_all[...], basis[...], NN)
+    remote(part.at[i], recv.at[i], send_sem.at[i], recv_sem.at[i], partner).start()
+
+    @pl.when(i == tiles - 1)
+    def _():
+        width = part.shape[2]
+        for j in range(tiles):
+            remote(part.at[j], recv.at[j], send_sem.at[j], recv_sem.at[j], partner).wait()
+            out[:, j * width:(j + 1) * width] = part[j] + recv[j]
+
+
+def rotate(q_all, basis_in, width):
+    depth, cols = basis_in.shape
+    rows = q_all.shape[0]
+    tiles = cols // width
+    dma = pltpu.SemaphoreType.DMA
+    return pl.pallas_call(
+        functools.partial(rotate_kernel, tiles),
+        grid=(tiles,),
+        out_shape=jax.ShapeDtypeStruct((rows, cols), F32),
+        in_specs=[
+            pl.BlockSpec((rows, depth), lambda i: (0, 0)),
+            pl.BlockSpec((depth, width), lambda i: (0, i)),
+        ],
+        out_specs=pl.BlockSpec((rows, cols), lambda i: (0, 0)),
+        scratch_shapes=[
+            pltpu.VMEM((tiles, rows, width), F32), pltpu.VMEM((tiles, rows, width), F32),
+            dma((tiles,)), dma((tiles,)),
+        ],
+        compiler_params=params(1),
+    )(q_all, basis_in)
+
+
+def sketch_kernel(
+    n, b_ref, bucket, sign, eig, a_ref, left, bs_hi, bs_lo, part, recv, whole, gram_mine, gram_theirs,
+    rs_send, rs_recv, ag_send, ag_recv, g_sem,
+):
+    i = pl.program_id(0)
+    d = lax.axis_index("dp")
+    partner = {"tensor": 1 - lax.axis_index("tensor")}
+
+    @pl.when(i == 0)
+    def _():
+        greet([{"dp": lax.rem(d + k, n)} for k in range(1, n)] + [partner])
+        signs = (2 * sign[...] - 1).astype(F32)
+        for k in range(RANK):
+            table = jnp.where(bucket[...] == k, signs, 0.0)
+            hi, lo = split(b_ref[...] * table)
+            bs_hi[k * HALF_TOK:(k + 1) * HALF_TOK, :] = hi
+            bs_lo[k * HALF_TOK:(k + 1) * HALF_TOK, :] = lo
+
+    r_hi, r_lo = split(1.0 / (eig[...].astype(F32) + DAMP))
+    prod = mm(bs_hi[...], r_hi, NT) + mm(bs_lo[...], r_hi, NT) + mm(bs_hi[...], r_lo, NT)
+    width = eig.shape[0]
+    for k in range(RANK):
+        block = prod[k * HALF_TOK:(k + 1) * HALF_TOK] * a_ref[...]
+        part[i, k * HALF_Q:(k + 1) * HALF_Q, :] = block.reshape(HALF_Q, QLEN, width).sum(axis=1)
+
+    def scatter(k):
+        to = lax.rem(d + k, n)
+        return remote(part.at[to], recv.at[k], rs_send.at[k], rs_recv.at[k], {"dp": to})
+
+    @pl.when(i != d)
+    def _():
+        k = lax.rem(i - d + n, n)
+        remote(part.at[i], recv.at[k], rs_send.at[k], rs_recv.at[k], {"dp": i}).start()
+
+    @pl.when(i == n - 1)
+    def _():
+        total = part[d]
+        for k in range(1, n):
+            scatter(k).wait_recv()
+            total = total + recv[k]
+        whole[d] = total
+        for k in range(1, n):
+            to = lax.rem(d + k, n)
+            remote(whole.at[d], whole.at[d], ag_send.at[k], ag_recv.at[k], {"dp": to}).start()
+        for k in range(1, n):
+            to, source = lax.rem(d + k, n), lax.rem(d + n - k, n)
+            remote(whole.at[d], whole.at[source], ag_send.at[k], ag_recv.at[k], {"dp": to}).wait()
+            scatter(k).wait_send()
+        rows = [
+            jnp.concatenate([whole[c, k * HALF_Q:(k + 1) * HALF_Q, :] for c in range(n)], axis=1)
+            for k in range(RANK)
+        ]
+        lane = lax.broadcasted_iota(jnp.int32, (HALF_Q, 128), 1)
+        packed = jnp.zeros((HALF_Q, 128), F32)
+        for r in range(RANK):
+            for k in range(r + 1):
+                dot = jnp.sum(rows[r] * rows[k], axis=1, keepdims=True)
+                packed = jnp.where(lane == r * RANK + k, dot, packed)
+        gram_mine[0:HALF_Q, :] = packed
+        gram_mine[HALF_Q:2 * HALF_Q, :] = packed
+        copy = remote(gram_mine, gram_theirs, g_sem.at[0], g_sem.at[1], partner)
+        copy.start()
+        copy.wait()
+        gram = gram_mine[0:HALF_Q, :] + gram_theirs[0:HALF_Q, :]
+        low = [[None] * RANK for _ in range(RANK)]
+        done = []
+        for r in range(RANK):
+            for k in range(r + 1):
+                value = gram[:, r * RANK + k:r * RANK + k + 1]
+                for m in range(k):
+                    value = value - low[r][m] * low[k][m]
+                low[r][k] = jnp.sqrt(value) if k == r else value / low[k][k]
+            row = rows[r]
+            for k in range(r):
+                row = row - low[r][k] * done[k]
+            row = row / low[r][r]
+            done.append(row)
+            left[r * HALF_Q:(r + 1) * HALF_Q, :] = row
+
+
+def sketch_left(n, b, bucket, sign, eigval, a):
+    own_rows, cols = eigval.shape
+    width = own_rows // n
+    toks = b.shape[0]
+    dma = pltpu.SemaphoreType.DMA
+    fixed = lambda i: (0, 0)
+    return pl.pallas_call(
+        functools.partial(sketch_kernel, n),
+        grid=(n,),
+        out_shape=jax.ShapeDtypeStruct((HALF_COLS, own_rows), F32),
+        in_specs=[
+            pl.BlockSpec((toks, cols), fixed),
+            pl.BlockSpec((1, cols), fixed),
+            pl.BlockSpec((1, cols), fixed),
+            pl.BlockSpec((width, cols), lambda i: (i, 0)),
+            pl.BlockSpec((toks, width), lambda i: (0, i)),
+        ],
+        out_specs=pl.BlockSpec((HALF_COLS, own_rows), fixed),
+        scratch_shapes=[
+            pltpu.VMEM((RANK * toks, cols), BF16), pltpu.VMEM((RANK * toks, cols), BF16),
+            pltpu.VMEM((n, HALF_COLS, width), F32), pltpu.VMEM((n, HALF_COLS, width), F32),
+            pltpu.VMEM((n, HALF_COLS, width), F32),
+            pltpu.VMEM((2 * HALF_Q, 128), F32), pltpu.VMEM((2 * HALF_Q, 128), F32),
+            dma((n,)), dma((n,)), dma((n,)), dma((n,)), dma((2,)),
+        ],
+        compiler_params=params(2),
+    )(b, bucket, sign, eigval, a)
+
+
+def right_kernel(tiles, left, a_ref, eig, b_ref, out, al_hi, al_lo, part, recv, send_sem, recv_sem):
+    i = pl.program_id(0)
+    partner = {"tensor": 1 - lax.axis_index("tensor")}
+    depth = left.shape[1]
+
+    @pl.when(i == 0)
+    def _():
+        greet([partner])
+        for r in range(RANK):
+            for j in range(HALF_Q):
+                at = r * HALF_Q + j
+                hi, lo = split(left[at:at + 1, :] * a_ref[j * QLEN:(j + 1) * QLEN, :])
+                al_hi[at * QLEN:(at + 1) * QLEN, :] = hi
+                al_lo[at * QLEN:(at + 1) * QLEN, :] = lo
+
+    r_hi, r_lo = split(1.0 / (eig[...].astype(F32) + DAMP))
+    prod = mm(al_hi[...], r_hi, NN) + mm(al_lo[...], r_hi, NN) + mm(al_hi[...], r_lo, NN)
+    width = eig.shape[1]
+    for r in range(RANK):
+        block = prod[r * HALF_TOK:(r + 1) * HALF_TOK] * b_ref[...]
+        part[i, r * HALF_Q:(r + 1) * HALF_Q, :] = block.reshape(HALF_Q, QLEN, width).sum(axis=1)
+    remote(part.at[i], recv.at[i], send_sem.at[i], recv_sem.at[i], partner).start()
+
+    @pl.when(i == tiles - 1)
+    def _():
+        for j in range(tiles):
+            remote(part.at[j], recv.at[j], send_sem.at[j], recv_sem.at[j], partner).wait()
+            out[:, j * width:(j + 1) * width] = part[j] + recv[j]
+
+
+def right_factors(left, a, eigval, b, width):
+    own_rows, cols = eigval.shape
+    tiles = cols // width
+    toks = b.shape[0]
+    dma = pltpu.SemaphoreType.DMA
+    fixed = lambda i: (0, 0)
+    return pl.pallas_call(
+        functools.partial(right_kernel, tiles),
+        grid=(tiles,),
+        out_shape=jax.ShapeDtypeStruct((HALF_COLS, cols), F32),
+        in_specs=[
+            pl.BlockSpec((HALF_COLS, own_rows), fixed),
+            pl.BlockSpec((toks, own_rows), fixed),
+            pl.BlockSpec((own_rows, width), lambda i: (0, i)),
+            pl.BlockSpec((toks, width), lambda i: (0, i)),
+        ],
+        out_specs=pl.BlockSpec((HALF_COLS, cols), fixed),
+        scratch_shapes=[
+            pltpu.VMEM((RANK * toks, own_rows), BF16), pltpu.VMEM((RANK * toks, own_rows), BF16),
+            pltpu.VMEM((tiles, HALF_COLS, width), F32), pltpu.VMEM((tiles, HALF_COLS, width), F32),
+            dma((tiles,)), dma((tiles,)),
+        ],
+        compiler_params=params(3),
+    )(left, a, eigval, b)
+
+
+def score_kernel(
+    n, basis_in, right, left, basis_out, train_out, train_in, member, lens, owner, scores, totals,
+    tile, part, recv, r_all, l_mine, l_theirs, l_all, proj, proj_theirs, src, src_recv, in_sem,
+    rs_send, rs_recv, r_send, r_recv, l_send, l_recv, x_sem, s_send, s_recv,
+):
+    d = lax.axis_index("dp")
+    p = lax.axis_index("pool")
+    t = lax.axis_index("tensor")
+    rows = tile.shape[1]
+    out_rows = basis_out.shape[0]
+    per_core = n // 2
+    partner = {"tensor": 1 - t}
+    peers = [lax.rem(d + k, n) for k in range(n)]
+    others = [
+        (q, k, {"pool": lax.rem(p + q, 2), "dp": peers[k]})
+        for k in range(n) for q in range(2) if (q, k) != (0, 0)
+    ]
+
+    def fetch(s):
+        to = lax.rem(d + 1 + s, n)
+        return pltpu.make_async_copy(
+            basis_in.at[pl.ds(pl.multiple_of(to * rows, rows), rows)], tile.at[s], in_sem.at[s]
+        )
+
+    for s in range(n):
+        fetch(s).start()
+    greet([target for _, _, target in others] + [partner])
+
+    left_hi, left_lo = split(left[...])
+    l_mine[...] = mm(left_hi, basis_out[...], NT) + mm(left_lo, basis_out[...], NT)
+    holds = d // per_core == t
+    handover = remote(l_mine, l_theirs, x_sem.at[0], x_sem.at[1], partner)
+
+    @pl.when(jnp.logical_not(holds))
+    def _():
+        handover.start()
+
+    right_hi, right_lo = split(right[...])
+    pad = jnp.zeros_like(right_hi)
+    stacked = jnp.concatenate([right_hi, right_lo, pad, pad], axis=0)
+
+    def scatter(k):
+        return remote(part.at[k - 1], recv.at[k], rs_send.at[k], rs_recv.at[k], {"dp": peers[k]})
+
+    def step(s, carry):
+        fetch(s).wait()
+        prod = jnp.transpose(mm(tile[s], stacked, NT))
+        part[s] = prod[:HALF_COLS] + prod[HALF_COLS:2 * HALF_COLS]
+
+        @pl.when(s < n - 1)
+        def _():
+            to = lax.rem(d + 1 + s, n)
+            remote(part.at[s], recv.at[s + 1], rs_send.at[s + 1], rs_recv.at[s + 1], {"dp": to}).start()
+
+        return carry
+
+    lax.fori_loop(0, n, step, 0)
+
+    def left_copy(q, k, target, pool, index):
+        return remote(
+            l_all.at[p, lax.rem(d, per_core)], l_all.at[pool, index],
+            l_send.at[q, k], l_recv.at[q, k], target,
+        )
+
+    @pl.when(holds)
+    def _():
+        handover.wait_recv()
+        l_all[p, lax.rem(d, per_core)] = l_mine[...] + l_theirs[...]
+        for q, k, target in others:
+            left_copy(q, k, target, p, lax.rem(d, per_core)).start()
+
+    total = part[n - 1]
+    for k in range(1, n):
+        scatter(k).wait_recv()
+        total = total + recv[k]
+    r_all[p, d] = total
+
+    def right_copy(q, k, target, pool, index):
+        return remote(r_all.at[p, d], r_all.at[pool, index], r_send.at[q, k], r_recv.at[q, k], target)
+
+    for q, k, target in others:
+        right_copy(q, k, target, p, d).start()
+
+    for q, k, target in others:
+        source = lax.rem(d + n - k, n)
+
+        @pl.when(source // per_core == t)
+        def _():
+            left_copy(q, k, target, lax.rem(p + q, 2), lax.rem(source, per_core)).wait_recv()
+
+    acc_out = [jnp.zeros((train_out.shape[0], HALF_COLS), F32) for _ in range(2)]
+    for q in range(2):
+        for c in range(per_core):
+            hi, lo = split(l_all[q, c])
+            x = train_out[:, c * out_rows:(c + 1) * out_rows]
+            acc_out[q] = acc_out[q] + mm(x, hi, NT) + mm(x, lo, NT)
+    for q in range(2):
+        proj[q] = acc_out[q]
+
+    for q, k, target in others:
+        source = lax.rem(d + n - k, n)
+        right_copy(q, k, target, lax.rem(p + q, 2), source).wait_recv()
+    acc_in = [jnp.zeros((train_in.shape[0], HALF_COLS), F32) for _ in range(2)]
+    for q in range(2):
+        for c in range(n):
+            hi, lo = split(r_all[q, c])
+            x = train_in[:, c * rows:(c + 1) * rows]
+            acc_in[q] = acc_in[q] + mm(x, hi, NT) + mm(x, lo, NT)
+    for q in range(2):
+        proj[2 + q] = acc_in[q]
+    swap = remote(proj, proj_theirs, x_sem.at[2], x_sem.at[3], partner)
+    swap.start()
+    swap.wait()
+
+    highest = lax.Precision.HIGHEST
+    result = jnp.zeros(scores.shape, F32)
+    for q in range(2):
+        prod = (proj[q] + proj_theirs[q]) * (proj[2 + q] + proj_theirs[2 + q])
+        by_col = jnp.dot(member[...], prod, precision=highest, preferred_element_type=F32)
+        col = lax.broadcasted_iota(jnp.int32, (HALF_COLS, scores.shape[1]), 0)
+        query = lax.broadcasted_iota(jnp.int32, (HALF_COLS, scores.shape[1]), 1)
+        j = col % HALF_Q
+        pick = (query == 2 * j + (j + q) % 2).astype(F32)
+        result = result + jnp.dot(by_col, pick, precision=highest, preferred_element_type=F32)
+    result = result / lens[...]
+    scores[...] = result
+    src[...] = jnp.dot(owner[...], result, precision=highest, preferred_element_type=F32)
+    for k in range(1, n):
+        remote(src, src_recv.at[k], s_send.at[k], s_recv.at[k], {"dp": peers[k]}).start()
+    out = src[...]
+    for k in range(1, n):
+        remote(src, src_recv.at[k], s_send.at[k], s_recv.at[k], {"dp": peers[k]}).wait()
+    for m in range(n):
+        k = lax.rem(d - m + n, n)
+        src_recv[0] = src[...]
+        out = src_recv[k] if m == 0 else out + src_recv[k]
+    totals[...] = out
+
+    for k in range(1, n):
+        scatter(k).wait_send()
+    for q, k, target in others:
+        right_copy(q, k, target, p, d).wait_send()
+
+    @pl.when(holds)
+    def _():
+        for q, k, target in others:
+            left_copy(q, k, target, p, lax.rem(d, per_core)).wait_send()
+
+    @pl.when(jnp.logical_not(holds))
+    def _():
+        handover.wait_send()
+
+
+def score(n, basis_in, right, left, basis_out, train_out, train_in, member, lens, owner):
+    rows = basis_in.shape[0] // n
+    toks = train_in.shape[0]
+    out_rows = basis_out.shape[0]
+    dma = pltpu.SemaphoreType.DMA
+    vm = pltpu.VMEM
+    return pl.pallas_call(
+        functools.partial(score_kernel, n),
+        out_shape=(
+            jax.ShapeDtypeStruct((member.shape[0], 128), F32),
+            jax.ShapeDtypeStruct((SOURCES, 128), F32),
+        ),
+        in_specs=[pl.BlockSpec(memory_space=pl.ANY)] + [VMEM] * 8,
+        out_specs=(VMEM, VMEM),
+        scratch_shapes=[
+            vm((n, rows, basis_in.shape[1]), BF16),
+            vm((n, HALF_COLS, rows), F32), vm((n, HALF_COLS, rows), F32),
+            vm((2, n, HALF_COLS, rows), F32),
+            vm((HALF_COLS, out_rows), F32), vm((HALF_COLS, out_rows), F32),
+            vm((2, n // 2, HALF_COLS, out_rows), F32),
+            vm((4, toks, HALF_COLS), F32), vm((4, toks, HALF_COLS), F32),
+            vm((SOURCES, 128), F32), vm((n, SOURCES, 128), F32),
+            dma((n,)), dma((n,)), dma((n,)), dma((2, n)), dma((2, n)), dma((2, n)), dma((2, n)),
+            dma((4,)), dma((n,)), dma((n,)),
+        ],
+        compiler_params=params(4),
+    )(basis_in, right, left, basis_out, train_out, train_in, member, lens, owner)
+
+
+def body(
+    n,
+    train_out,
+    train_in,
+    query_out,
+    query_in,
+    basis_out,
+    basis_in,
+    eigval,
+    sketch_bucket,
+    sketch_sign,
+    lengths,
+    source_of_seq,
+):
+    p = lax.axis_index("pool")
+    pairs = query_out.reshape(HALF_Q, 2, QLEN, query_out.shape[1])
+    odd = ((jnp.arange(HALF_Q, dtype=jnp.int32) + p) % 2)[:, None, None]
+    own_query_out = jnp.where(odd == 0, pairs[:, 0], pairs[:, 1]).reshape(HALF_TOK, -1)
+    out_part = jnp.dot(own_query_out, basis_out, preferred_element_type=F32)
+    q_all, a = gather(n, query_in, out_part)
+    b = rotate(q_all, basis_in, 256)
+    left = sketch_left(n, b, sketch_bucket[None], sketch_sign[None], eigval, a)
+    right = right_factors(left, a, eigval, b, 256)
+
+    seqs = lengths.shape[1]
+    toks = train_out.shape[0]
+    seq_len = lengths[0]
+    seq_ends = jnp.cumsum(seq_len)
+    seq_starts = seq_ends - seq_len
+    positions = jnp.arange(toks, dtype=jnp.int32)
+    member = (
+        (positions[None, :] >= seq_starts[:, None]) & (positions[None, :] < seq_ends[:, None])
+    ).astype(F32)
+    pad_rows = 8 - seqs
+    member = jnp.pad(member, ((0, pad_rows), (0, 0)))
+    lens = jnp.pad(seq_len.astype(F32)[:, None], ((0, pad_rows), (0, 0)), constant_values=1.0)
+    owner = (source_of_seq[None, :] == jnp.arange(SOURCES, dtype=jnp.int32)[:, None]).astype(F32)
+    owner = jnp.pad(owner, ((0, 0), (0, pad_rows)))
+    scores, totals = score(n, basis_in, right, left, basis_out, train_out, train_in, member, lens, owner)
+    return (scores[:seqs, :QUERIES], totals[:, :QUERIES])
 
 
 def sketch_table(bucket_ids, sign_bits):
@@ -27,7 +578,7 @@
     return jnp.dot(member, token_score, precision=lax.Precision.HIGHEST)
 
 
-def body(
+def wide_body(
     train_out,
     train_in,
     query_out,
@@ -101,8 +652,10 @@
 
 
 def solution(mesh):
+    n = mesh.shape["dp"]
+    small = mesh.shape["pool"] == 2 and mesh.shape["tensor"] == 2 and n == QUERIES
     return jax.shard_map(
-        body,
+        functools.partial(body, n) if small else wide_body,
         mesh=mesh,
         in_specs=(
             P(("pool", "dp"), "tensor"),

time: 766 us -> 229 us (0.30)
  waiting for transfers between devices: 370 us -> 0 us
  matrix products: 327 us -> 2.86 us
  Pallas kernels: 0 us -> 218 us
  blocking collectives: 25.6 us -> 0 us
  other arithmetic: 22.7 us -> 1.58 us
  between operations: 14.7 us -> 0.74 us
    dot_general x12 -> x1, matrix products: 326 us -> 2.86 us  [body(): out_part = jnp.dot(own_query_out, basis_out, preferred_element_type=F32)]
    psum x6 -> x0, waiting for transfers between devices: 283 us -> none  [the longest x1 96 us: body(): right_full = lax.psum(right_term, 'dp')]
    pallas_call x0 -> x5, Pallas kernels: none -> 218 us  [the longest x1 95.7 us: score(): pl.pallas_call(functools.partial(score_kernel, n), out_shape=(jax.ShapeDt...]
    all_gather x2 -> x0, waiting for transfers between devices: 84.7 us -> none  [the longest x1 47.3 us: body(): lax.all_gather(query_in, 'dp', axis=0, tiled=True)]
    psum x2 -> x0, blocking collectives: 25.6 us -> none  [the longest x1 22.2 us: body(): source_totals = lax.psum(source_part, 'dp')]
    another operation x8 -> x1, other arithmetic: 11.6 us -> 0.18 us  [the longest x4 6.28 us: body(): chol_factor = jnp.linalg.cholesky(gram_matrix)]
    add x1 -> x0, other arithmetic: 9.63 us -> none  [body(): eig_plus = eigval.astype(jnp.float32) + DAMP]
  transfers between devices with their start and end apart: 8 -> 0, of which waited for: 8 -> 0; matrix products, arithmetic and copies ran while one was open for 4% -> 0% of each run, Pallas kernels for 0% -> 0%
where the time goes in v1:
time: 229 us
  Pallas kernels  218 us (95%)
  local copies, waits for them, and re-layouts  5.58 us (2%)
  matrix products  2.86 us (1%)
    pallas_call x1, Pallas kernels, score(): pl.pallas_call(functools.partial(score_kernel, n), out_shape=(jax.ShapeDt...  95.7 us
    pallas_call x1, Pallas kernels, gather(): pl.pallas_call(functools.partial(gather_kernel, n), out_shape=(jax.ShapeD...  55.1 us
    pallas_call x1, Pallas kernels, sketch_left(): pl.pallas_call(functools.partial(sketch_kernel, n), grid=(n,), out_shape=...  36 us
    pallas_call x1, Pallas kernels, right_factors(): pl.pallas_call(functools.partial(right_kernel, tiles), grid=(tiles,), out...  17.3 us
    pallas_call x1, Pallas kernels, rotate(): pl.pallas_call(functools.partial(rotate_kernel, tiles), grid=(tiles,), ou...  13.9 us

profile of v1, /device:TPU:0, one launch (start us, length us, event | category | flops | bytes accessed | tf_op | source)
XLA Modules:
  0.0 228.8 jit_solution(14172430936512789638)
XLA Ops:
  0.6 0.9 fusion.3
  1.5 0.1 broadcast_in_dim.26
  1.6 0.1 broadcast_in_dim.27
  1.7 0.1 bitcast_select_fusion
  1.8 2.9 %fusion.4.part = f32[64,2048]{1,0:T(8,128)} fusion(bf16[64,512]{1,0:T(8,128)(2,1)S(1)} %bitcast_select_fusion, bf16[512,2048]{1,0:T(8,128)(2,1)} %basis_out.1), kind=kOutput, calls=%fused_computation.14 | convolution fusion | flops 134217728 | bytes 2686976 | tf_op jit(solution)/shard_map/dot_general | solution.py:542
  4.7 55.1 %shard_map.122 = (bf16[64,7168]{1,0:T(8,128)(2,1)}, f32[64,2048]{1,0:T(8,128)}) custom-call(bf16[16,7168]{1,0:T(8,128)(2,1)} %qin.1, f32[64,2048]{1,0:T(8,128)} %fusion.4.part), custom_call_target="tpu_custom_call" | custom-call | tf_op jit(solution)/shard_map/pallas_call | solution.py:120
  59.8 0.0 copy-start
  59.8 0.0 copy-start.1
  59.8 13.9 %shard_map.123.b_ref = f32[64,1792]{1,0:T(8,128)} custom-call(bf16[64,7168]{1,0:T(8,128)(2,1)} %get-tuple-element.6.q_all, bf16[7168,1792]{1,0:T(8,128)(2,1)} %basis_in.1), custom_call_target="tpu_custom_call" | custom-call | tf_op jit(solution)/shard_map/pallas_call | solution.py:160
  73.7 0.6 broadcast_in_dim.29.bucket
  74.4 0.6 broadcast_in_dim.30.sign
  74.9 36.0 %shard_map.124.left = f32[32,2048]{1,0:T(8,128)} custom-call(f32[64,1792]{1,0:T(8,128)} %shard_map.123.b_ref, s32[1,1792]{1,0:T(1,128)} %broadcast_in_dim.29.bucket, s32[1,1792]{1,0:T(1,128)} %broadcast_in_dim.30.sign, bf16[2048,1792]{1,0:T(8,128)(2,1)} %eig.3, f32[64,2048]{1,0:T(8,128)} %get-tuple-element.7.a_ref), custom_call_target="tpu_custom_call" | custom-call | tf_op jit(solution)/shard_map/pallas_call | solution.py:263
  111.0 0.0 copy-start.2
  111.0 0.0 copy-start.3
  111.0 17.3 %shard_map.125.right = f32[32,1792]{1,0:T(8,128)} custom-call(f32[32,2048]{1,0:T(8,128)} %shard_map.124.left, f32[64,2048]{1,0:T(8,128)} %get-tuple-element.7.a_ref, bf16[2048,1792]{1,0:T(8,128)(2,1)} %eig.3, f32[64,1792]{1,0:T(8,128)} %shard_map.123.b_ref), custom_call_target="tpu_custom_call" | custom-call | tf_op jit(solution)/shard_map/pallas_call | solution.py:322
  128.4 0.2 reduce-window.7
  128.6 0.1 fusion
  128.6 0.6 pad_convert_fusion.1.member
  129.2 0.1 copy.13
  129.3 0.6 pad.18.lens
  129.9 0.6 pad_convert_fusion.owner
  130.6 95.7 %shard_map.126 = (f32[8,128]{1,0:T(8,128)}, f32[32,128]{1,0:T(8,128)}) custom-call(bf16[7168,1792]{1,0:T(8,128)(2,1)} %basis_in.1, f32[32,1792]{1,0:T(8,128)} %shard_map.125.right, f32[32,2048]{1,0:T(8,128)} %shard_map.124.left, bf16[512,2048]{1,0:T(8,128)(2,1)} %basis_out.1, bf16[128,2048]{1,0:T(8,128)(2,1)} %train_out.1, bf16[128,7168]{1,0:T(8,128)(2,1)} %train_in.1, ...), custom_call_target="tpu_custom_call" | custom-call | tf_op jit(solution)/shard_map/pallas_call | solution.py:501
  226.2 1.4 copy.14
  227.6 1.2 slice.14
  (8 shorter events, 0.0 us)
Async XLA Ops:
  59.8 14.0 %copy-start = (s32[1792]{0:T(1024)S(1)}, s32[1792]{0:T(1024)}, u32[]{:S(2)}) copy-start(s32[1792]{0:T(1024)} %param.18) | copy-start | bytes 21508
  59.8 14.6 %copy-start.1 = (s32[1792]{0:T(1024)S(1)}, s32[1792]{0:T(1024)}, u32[]{:S(2)}) copy-start(s32[1792]{0:T(1024)} %param.19) | copy-start | bytes 21508
  111.0 17.4 %copy-start.2 = (s32[1,4]{1,0:T(1,128)S(1)}, s32[1,4]{1,0:T(1,128)}, u32[]{:S(2)}) copy-start(s32[1,4]{1,0:T(1,128)} %param.20) | copy-start | bytes 52
  111.0 18.9 %copy-start.3 = (s32[4]{0:T(128)S(1)}, s32[4]{0:T(128)}, u32[]{:S(2)}) copy-start(s32[4]{0:T(128)} %param.21) | copy-start | bytes 52

commit v2 on v1

--- a/solution.py
+++ b/solution.py
@@ -55,94 +55,123 @@
     )
 
 
-def gather_kernel(n, qin, part, q_all, a_out, recv, q_send, q_recv, rs_send, rs_recv, ag_send, ag_recv):
+def other_devices(n):
     d = lax.axis_index("dp")
     p = lax.axis_index("pool")
-    rows = part.shape[0] // n
+    return [
+        (q, k, {"pool": lax.rem(p + q, 2), "dp": lax.rem(d + k, n)})
+        for k in range(n) for q in range(2) if (q, k) != (0, 0)
+    ]
+
+
+def gather_kernel(zs, qin, qout, basis, q_all, part, z_send, z_recv, x_send, x_recv):
+    d = lax.axis_index("dp")
+    p = lax.axis_index("pool")
+    z, x = d // 2, d % 2
+    across = {"dp": 2 * z + 1 - x}
+    greet([{"dp": 2 * lax.rem(z + k, zs) + x} for k in range(1, zs)] + [across])
+    own = pl.ds(pl.multiple_of(z * QLEN, QLEN), QLEN)
+    is_sender = x == lax.rem(z + p, 2)
+
+    def along(k):
+        return remote(qin, q_all.at[own], z_send.at[k], z_recv.at[z], {"dp": 2 * lax.rem(z + k, zs) + x})
+
+    def over(j):
+        rows = q_all.at[j * QLEN:(j + 1) * QLEN]
+        return remote(rows, rows, x_send.at[j], x_recv.at[j], across)
+
+    @pl.when(is_sender)
+    def _():
+        for k in range(1, zs):
+            along(k).start()
+        q_all[own, :] = qin[...]
+
+    part[...] = mm(qout[...], basis[...], NN)
+    for j in range(zs):
+        in_column = x == lax.rem(j + p, 2)
+
+        @pl.when(jnp.logical_and(in_column, z != j))
+        def _():
+            rows = q_all.at[j * QLEN:(j + 1) * QLEN]
+            remote(qin, rows, z_send.at[0], z_recv.at[j], across).wait_recv()
+
+        @pl.when(in_column)
+        def _():
+            over(j).start()
+
+    for j in range(zs):
+        in_column = x == lax.rem(j + p, 2)
+
+        @pl.when(in_column)
+        def _():
+            over(j).wait_send()
+
+        @pl.when(jnp.logical_not(in_column))
+        def _():
+            over(j).wait_recv()
+
+    @pl.when(is_sender)
+    def _():
+        for k in range(1, zs):
+            along(k).wait_send()
+
+
+def gather(n, query_in, query_out, basis_out):
+    dma = pltpu.SemaphoreType.DMA
+    zs = n // 2
+    return pl.pallas_call(
+        functools.partial(gather_kernel, zs),
+        out_shape=(
+            jax.ShapeDtypeStruct((HALF_TOK, query_in.shape[1]), BF16),
+            jax.ShapeDtypeStruct((HALF_TOK, basis_out.shape[1]), F32),
+        ),
+        in_specs=[VMEM] * 3,
+        out_specs=(VMEM, VMEM),
+        scratch_shapes=[dma((zs,)), dma((zs,)), dma((zs,)), dma((zs,))],
+        compiler_params=params(0),
+    )(query_in, query_out, basis_out)
+
+
+def rotate_kernel(
+    n, tiles, q_all, basis, a_in, out, a_out, part, recv, a_part, a_sum, a_recv, send_sem, recv_sem,
+    rs_send, rs_recv, ag_send, ag_recv,
+):
+    i = pl.program_id(0)
+    d = lax.axis_index("dp")
+    partner = {"tensor": 1 - lax.axis_index("tensor")}
     peers = [lax.rem(d + k, n) for k in range(n)]
-    greet([{"dp": peers[k]} for k in range(1, n)])
+    rows = a_part.shape[0] // n
+    own = pl.ds(pl.multiple_of(d * rows, rows), rows)
 
     def scatter(k):
         return remote(
-            part.at[pl.ds(pl.multiple_of(peers[k] * rows, rows), rows)], recv.at[k],
+            a_part.at[pl.ds(pl.multiple_of(peers[k] * rows, rows), rows)], a_recv.at[k],
             rs_send.at[k], rs_recv.at[k], {"dp": peers[k]},
         )
 
-    for k in range(1, n):
-        scatter(k).start()
-    mine = d // 2
-    is_sender = d == 2 * mine + lax.rem(mine + p, 2)
-
-    def query_copy(j, k):
-        return remote(
-            qin, q_all.at[pl.ds(pl.multiple_of(j * QLEN, QLEN), QLEN)],
-            q_send.at[k], q_recv.at[j], {"dp": peers[k]},
-        )
-
-    @pl.when(is_sender)
-    def _():
+    def share(k, source):
+        theirs = pl.ds(pl.multiple_of(source * rows, rows), rows)
+        return remote(a_sum.at[own], a_sum.at[theirs], ag_send.at[k], ag_recv.at[k], {"dp": peers[k]})
+
+    @pl.when(i == 0)
+    def _():
+        greet([partner] + [{"dp": peers[k]} for k in range(1, n)])
+        a_part[...] = a_in[...]
         for k in range(1, n):
-            query_copy(mine, k).start()
-        q_all[pl.ds(pl.multiple_of(mine * QLEN, QLEN), QLEN), :] = qin[...]
-
-    for k in range(1, n):
-        scatter(k).wait_recv()
-    own = pl.ds(pl.multiple_of(d * rows, rows), rows)
-    total = part[own, :]
-    for k in range(1, n):
-        total = total + recv[k]
-    a_out[own, :] = total
-
-    def share(k):
-        return remote(a_out.at[own], a_out.at[own], ag_send.at[k], ag_recv.at[k], {"dp": peers[k]})
-
-    for k in range(1, n):
-        share(k).start()
-    for k in range(1, n):
-        source = lax.rem(d + n - k, n)
-        theirs = pl.ds(pl.multiple_of(source * rows, rows), rows)
-        remote(a_out.at[own], a_out.at[theirs], ag_send.at[k], ag_recv.at[k], {"dp": peers[k]}).wait_recv()
-        scatter(k).wait_send()
-        share(k).wait_send()
-    for j in range(HALF_Q):
-        @pl.when(d != 2 * j + lax.rem(j + p, 2))
-        def _():
-            query_copy(j, 1).wait_recv()
-
-    @pl.when(is_sender)
-    def _():
-        for k in range(1, n):
-            query_copy(mine, k).wait_send()
-
-
-def gather(n, query_in, out_part):
-    dma = pltpu.SemaphoreType.DMA
-    return pl.pallas_call(
-        functools.partial(gather_kernel, n),
-        out_shape=(
-            jax.ShapeDtypeStruct((HALF_TOK, query_in.shape[1]), BF16),
-            jax.ShapeDtypeStruct(out_part.shape, F32),
-        ),
-        in_specs=[VMEM] * 2,
-        out_specs=(VMEM, VMEM),
-        scratch_shapes=[
-            pltpu.VMEM((n, out_part.shape[0] // n, out_part.shape[1]), F32),
-            dma((n,)), dma((HALF_Q,)), dma((n,)), dma((n,)), dma((n,)), dma((n,)),
-        ],
-        compiler_params=params(0),
-    )(query_in, out_part)
-
-
-def rotate_kernel(tiles, q_all, basis, out, part, recv, send_sem, recv_sem):
-    i = pl.program_id(0)
-    partner = {"tensor": 1 - lax.axis_index("tensor")}
-
-    @pl.when(i == 0)
-    def _():
-        greet([partner])
+            scatter(k).start()
 
     part[i] = mm(q_all[...], basis[...], NN)
     remote(part.at[i], recv.at[i], send_sem.at[i], recv_sem.at[i], partner).start()
+
+    @pl.when(i == tiles // 2)
+    def _():
+        total = a_part[own, :]
+        for k in range(1, n):
+            scatter(k).wait_recv()
+            total = total + a_recv[k]
+        a_sum[own, :] = total
+        for k in range(1, n):
+            share(k, d).start()
 
     @pl.when(i == tiles - 1)
     def _():
@@ -150,28 +179,39 @@
         for j in range(tiles):
             remote(part.at[j], recv.at[j], send_sem.at[j], recv_sem.at[j], partner).wait()
             out[:, j * width:(j + 1) * width] = part[j] + recv[j]
-
-
-def rotate(q_all, basis_in, width):
+        for k in range(1, n):
+            share(k, lax.rem(d + n - k, n)).wait()
+            scatter(k).wait_send()
+        a_out[...] = a_sum[...]
+
+
+def rotate(n, q_all, basis_in, a_part, width):
     depth, cols = basis_in.shape
     rows = q_all.shape[0]
     tiles = cols // width
     dma = pltpu.SemaphoreType.DMA
+    fixed = lambda i: (0, 0)
     return pl.pallas_call(
-        functools.partial(rotate_kernel, tiles),
+        functools.partial(rotate_kernel, n, tiles),
         grid=(tiles,),
-        out_shape=jax.ShapeDtypeStruct((rows, cols), F32),
+        out_shape=(
+            jax.ShapeDtypeStruct((rows, cols), F32),
+            jax.ShapeDtypeStruct(a_part.shape, F32),
+        ),
         in_specs=[
-            pl.BlockSpec((rows, depth), lambda i: (0, 0)),
+            pl.BlockSpec((rows, depth), fixed),
             pl.BlockSpec((depth, width), lambda i: (0, i)),
+            VMEM,
         ],
-        out_specs=pl.BlockSpec((rows, cols), lambda i: (0, 0)),
+        out_specs=(pl.BlockSpec((rows, cols), fixed), VMEM),
         scratch_shapes=[
             pltpu.VMEM((tiles, rows, width), F32), pltpu.VMEM((tiles, rows, width), F32),
-            dma((tiles,)), dma((tiles,)),
+            pltpu.VMEM(a_part.shape, F32), pltpu.VMEM(a_part.shape, F32),
+            pltpu.VMEM((n, a_part.shape[0] // n, a_part.shape[1]), F32),
+            dma((tiles,)), dma((tiles,)), dma((n,)), dma((n,)), dma((n,)), dma((n,)),
         ],
         compiler_params=params(1),
-    )(q_all, basis_in)
+    )(q_all, basis_in, a_part)
 
 
 def sketch_kernel(
@@ -283,14 +323,36 @@
     )(b, bucket, sign, eigval, a)
 
 
-def right_kernel(tiles, left, a_ref, eig, b_ref, out, al_hi, al_lo, part, recv, send_sem, recv_sem):
+def right_kernel(
+    n, tiles, left, a_ref, basis_out, eig, b_ref, out, l_out, al_hi, al_lo, part, recv, l_mine, l_theirs, l_all,
+    send_sem, recv_sem, l_send, l_recv, x_sem,
+):
     i = pl.program_id(0)
-    partner = {"tensor": 1 - lax.axis_index("tensor")}
-    depth = left.shape[1]
+    d = lax.axis_index("dp")
+    p = lax.axis_index("pool")
+    t = lax.axis_index("tensor")
+    partner = {"tensor": 1 - t}
+    per_core = n // 2
+    others = other_devices(n)
+    holds = d // per_core == t
+    handover = remote(l_mine, l_theirs, x_sem.at[0], x_sem.at[1], partner)
+
+    def left_copy(q, k, target, pool, index):
+        return remote(
+            l_all.at[p, lax.rem(d, per_core)], l_all.at[pool, index],
+            l_send.at[q, k], l_recv.at[q, k], target,
+        )
 
     @pl.when(i == 0)
     def _():
-        greet([partner])
+        greet([target for _, _, target in others] + [partner])
+        left_hi, left_lo = split(left[...])
+        l_mine[...] = mm(left_hi, basis_out[...], NT) + mm(left_lo, basis_out[...], NT)
+
+        @pl.when(jnp.logical_not(holds))
+        def _():
+            handover.start()
+
         for r in range(RANK):
             for j in range(HALF_Q):
                 at = r * HALF_Q + j
@@ -306,150 +368,201 @@
         part[i, r * HALF_Q:(r + 1) * HALF_Q, :] = block.reshape(HALF_Q, QLEN, width).sum(axis=1)
     remote(part.at[i], recv.at[i], send_sem.at[i], recv_sem.at[i], partner).start()
 
+    @pl.when(jnp.logical_and(i == 0, holds))
+    def _():
+        handover.wait_recv()
+        l_all[p, lax.rem(d, per_core)] = l_mine[...] + l_theirs[...]
+        for q, k, target in others:
+            left_copy(q, k, target, p, lax.rem(d, per_core)).start()
+
     @pl.when(i == tiles - 1)
     def _():
+        for q, k, target in others:
+            source = lax.rem(d + n - k, n)
+
+            @pl.when(source // per_core == t)
+            def _():
+                left_copy(q, k, target, lax.rem(p + q, 2), lax.rem(source, per_core)).wait_recv()
+
+            @pl.when(holds)
+            def _():
+                left_copy(q, k, target, p, lax.rem(d, per_core)).wait_send()
+
+        @pl.when(jnp.logical_not(holds))
+        def _():
+            handover.wait_send()
+
+        l_out[...] = l_all[...]
         for j in range(tiles):
             remote(part.at[j], recv.at[j], send_sem.at[j], recv_sem.at[j], partner).wait()
             out[:, j * width:(j + 1) * width] = part[j] + recv[j]
 
 
-def right_factors(left, a, eigval, b, width):
+def right_factors(n, left, a, basis_out, eigval, b, width):
     own_rows, cols = eigval.shape
     tiles = cols // width
     toks = b.shape[0]
     dma = pltpu.SemaphoreType.DMA
     fixed = lambda i: (0, 0)
     return pl.pallas_call(
-        functools.partial(right_kernel, tiles),
+        functools.partial(right_kernel, n, tiles),
         grid=(tiles,),
-        out_shape=jax.ShapeDtypeStruct((HALF_COLS, cols), F32),
+        out_shape=(
+            jax.ShapeDtypeStruct((HALF_COLS, cols), F32),
+            jax.ShapeDtypeStruct((2, n // 2, HALF_COLS, basis_out.shape[0]), F32),
+        ),
         in_specs=[
             pl.BlockSpec((HALF_COLS, own_rows), fixed),
             pl.BlockSpec((toks, own_rows), fixed),
+            VMEM,
             pl.BlockSpec((own_rows, width), lambda i: (0, i)),
             pl.BlockSpec((toks, width), lambda i: (0, i)),
         ],
-        out_specs=pl.BlockSpec((HALF_COLS, cols), fixed),
+        out_specs=(pl.BlockSpec((HALF_COLS, cols), fixed), VMEM),
         scratch_shapes=[
             pltpu.VMEM((RANK * toks, own_rows), BF16), pltpu.VMEM((RANK * toks, own_rows), BF16),
             pltpu.VMEM((tiles, HALF_COLS, width), F32), pltpu.VMEM((tiles, HALF_COLS, width), F32),
-            dma((tiles,)), dma((tiles,)),
+            pltpu.VMEM((HALF_COLS, basis_out.shape[0]), F32),
+            pltpu.VMEM((HALF_COLS, basis_out.shape[0]), F32),
+            pltpu.VMEM((2, n // 2, HALF_COLS, basis_out.shape[0]), F32),
+            dma((tiles,)), dma((tiles,)), dma((2, n)), dma((2, n)), dma((2,)),
         ],
         compiler_params=params(3),
-    )(left, a, eigval, b)
+    )(left, a, basis_out, eigval, b)
 
 
 def score_kernel(
-    n, basis_in, right, left, basis_out, train_out, train_in, member, lens, owner, scores, totals,
-    tile, part, recv, r_all, l_mine, l_theirs, l_all, proj, proj_theirs, src, src_recv, in_sem,
-    rs_send, rs_recv, r_send, r_recv, l_send, l_recv, x_sem, s_send, s_recv,
+    n, basis_in, right, l_all, train_out, train_in, member, lens, owner, scores, totals,
+    tile, part, recv_x, recv_z, r_all, proj, proj_theirs, src, src_recv, in_sem,
+    xs_send, xs_recv, zs_send, zs_recv, z_send, z_recv, x_send, x_recv, y_send, y_recv, w_send, w_recv,
+    t_sem, s_send, s_recv,
 ):
     d = lax.axis_index("dp")
     p = lax.axis_index("pool")
-    t = lax.axis_index("tensor")
     rows = tile.shape[1]
-    out_rows = basis_out.shape[0]
-    per_core = n // 2
-    partner = {"tensor": 1 - t}
+    out_rows = l_all.shape[3]
+    zs = n // 2
+    z, x = d // 2, d % 2
+    partner = {"tensor": 1 - lax.axis_index("tensor")}
+    across = {"dp": 2 * z + 1 - x}
+    beside = {"pool": 1 - p}
     peers = [lax.rem(d + k, n) for k in range(n)]
-    others = [
-        (q, k, {"pool": lax.rem(p + q, 2), "dp": peers[k]})
-        for k in range(n) for q in range(2) if (q, k) != (0, 0)
-    ]
+    up = [{"dp": 2 * lax.rem(z + k, zs) + x} for k in range(zs)]
 
     def fetch(s):
-        to = lax.rem(d + 1 + s, n)
+        side = jnp.where(s < zs, 1 - x, x)
+        to = 2 * lax.rem(z + 1 + s, zs) + side
         return pltpu.make_async_copy(
             basis_in.at[pl.ds(pl.multiple_of(to * rows, rows), rows)], tile.at[s], in_sem.at[s]
         )
 
     for s in range(n):
         fetch(s).start()
-    greet([target for _, _, target in others] + [partner])
-
-    left_hi, left_lo = split(left[...])
-    l_mine[...] = mm(left_hi, basis_out[...], NT) + mm(left_lo, basis_out[...], NT)
-    holds = d // per_core == t
-    handover = remote(l_mine, l_theirs, x_sem.at[0], x_sem.at[1], partner)
-
-    @pl.when(jnp.logical_not(holds))
-    def _():
-        handover.start()
+    greet([{"dp": peers[k]} for k in range(1, n)] + [beside, partner])
 
     right_hi, right_lo = split(right[...])
     pad = jnp.zeros_like(right_hi)
     stacked = jnp.concatenate([right_hi, right_lo, pad, pad], axis=0)
 
-    def scatter(k):
-        return remote(part.at[k - 1], recv.at[k], rs_send.at[k], rs_recv.at[k], {"dp": peers[k]})
-
-    def step(s, carry):
+    def share(s):
         fetch(s).wait()
         prod = jnp.transpose(mm(tile[s], stacked, NT))
-        part[s] = prod[:HALF_COLS] + prod[HALF_COLS:2 * HALF_COLS]
-
-        @pl.when(s < n - 1)
+        return prod[:HALF_COLS] + prod[HALF_COLS:2 * HALF_COLS]
+
+    def pass_over(s):
+        return remote(part.at[s], recv_x.at[s], xs_send.at[s], xs_recv.at[s], across)
+
+    def pass_along(m, target):
+        return remote(part.at[zs + m], recv_z.at[m], zs_send.at[m], zs_recv.at[m], target)
+
+    def first(s, carry):
+        part[s] = share(s)
+        pass_over(s).start()
+        return carry
+
+    lax.fori_loop(0, zs, first, 0)
+
+    def second(m, carry):
+        mine = share(zs + m)
+        pass_over(m).wait_recv()
+        part[zs + m] = mine + recv_x[m]
+
+        @pl.when(m < zs - 1)
         def _():
-            to = lax.rem(d + 1 + s, n)
-            remote(part.at[s], recv.at[s + 1], rs_send.at[s + 1], rs_recv.at[s + 1], {"dp": to}).start()
+            pass_along(m, {"dp": 2 * lax.rem(z + 1 + m, zs) + x}).start()
 
         return carry
 
-    lax.fori_loop(0, n, step, 0)
-
-    def left_copy(q, k, target, pool, index):
-        return remote(
-            l_all.at[p, lax.rem(d, per_core)], l_all.at[pool, index],
-            l_send.at[q, k], l_recv.at[q, k], target,
-        )
-
-    @pl.when(holds)
-    def _():
-        handover.wait_recv()
-        l_all[p, lax.rem(d, per_core)] = l_mine[...] + l_theirs[...]
-        for q, k, target in others:
-            left_copy(q, k, target, p, lax.rem(d, per_core)).start()
-
-    total = part[n - 1]
-    for k in range(1, n):
-        scatter(k).wait_recv()
-        total = total + recv[k]
-    r_all[p, d] = total
-
-    def right_copy(q, k, target, pool, index):
-        return remote(r_all.at[p, d], r_all.at[pool, index], r_send.at[q, k], r_recv.at[q, k], target)
-
-    for q, k, target in others:
-        right_copy(q, k, target, p, d).start()
-
-    for q, k, target in others:
-        source = lax.rem(d + n - k, n)
-
-        @pl.when(source // per_core == t)
-        def _():
-            left_copy(q, k, target, lax.rem(p + q, 2), lax.rem(source, per_core)).wait_recv()
+    lax.fori_loop(0, zs, second, 0)
 
     acc_out = [jnp.zeros((train_out.shape[0], HALF_COLS), F32) for _ in range(2)]
     for q in range(2):
-        for c in range(per_core):
+        for c in range(zs):
             hi, lo = split(l_all[q, c])
-            x = train_out[:, c * out_rows:(c + 1) * out_rows]
-            acc_out[q] = acc_out[q] + mm(x, hi, NT) + mm(x, lo, NT)
+            cols = train_out[:, c * out_rows:(c + 1) * out_rows]
+            acc_out[q] = acc_out[q] + mm(cols, hi, NT) + mm(cols, lo, NT)
+        proj[q] = acc_out[q]
+
+    total = part[n - 1]
+    for m in range(zs - 1):
+        pass_along(m, up[m + 1]).wait_recv()
+        total = total + recv_z[m]
+    r_all[p, d] = total
+
+    def block(pool, k, side):
+        return r_all.at[pool, 2 * lax.rem(z + zs - k, zs) + side]
+
+    def along(k, source):
+        return remote(r_all.at[p, d], source, z_send.at[k], z_recv.at[k], up[k])
+
+    def over(k, side):
+        return remote(block(p, k, side), block(p, k, side), x_send.at[k], x_recv.at[k], across)
+
+    def cross(k, pool):
+        return remote(block(pool, k, x), block(pool, k, x), y_send.at[k], y_recv.at[k], beside)
+
+    def corner(k, sending):
+        if k < zs // 2:
+            ref = block(1 - p, k, x if sending else 1 - x)
+            return remote(ref, ref, w_send.at[k], w_recv.at[k], across)
+        ref = block(p if sending else 1 - p, k, 1 - x)
+        return remote(ref, ref, w_send.at[k], w_recv.at[k], beside)
+
+    for k in range(1, zs):
+        along(k, r_all.at[p, d]).start()
+    for k in range(zs):
+        if k:
+            along(k, block(p, k, x)).wait_recv()
+        over(k, x).start()
+        cross(k, p).start()
+    acc_in = [jnp.zeros((train_in.shape[0], HALF_COLS), F32) for _ in range(2)]
+
+    def project(q, pool_at, dp_at, acc):
+        hi, lo = split(r_all[pool_at, dp_at])
+        cols = train_in[:, pl.ds(pl.multiple_of(dp_at * rows, rows), rows)]
+        return acc + mm(cols, hi, NT) + mm(cols, lo, NT)
+
+    for k in range(zs):
+        if k < zs // 2:
+            cross(k, 1 - p).wait_recv()
+            corner(k, True).start()
+            over(k, 1 - x).wait_recv()
+        else:
+            over(k, 1 - x).wait_recv()
+            corner(k, True).start()
+            cross(k, 1 - p).wait_recv()
+    for k in range(zs):
+        at = 2 * lax.rem(z + zs - k, zs)
+        acc_in[0] = project(0, p, at + x, acc_in[0])
+        acc_in[0] = project(0, p, at + 1 - x, acc_in[0])
+        acc_in[1] = project(1, 1 - p, at + x, acc_in[1])
+    for k in range(zs):
+        at = 2 * lax.rem(z + zs - k, zs)
+        corner(k, False).wait_recv()
+        acc_in[1] = project(1, 1 - p, at + 1 - x, acc_in[1])
     for q in range(2):
-        proj[q] = acc_out[q]
-
-    for q, k, target in others:
-        source = lax.rem(d + n - k, n)
-        right_copy(q, k, target, lax.rem(p + q, 2), source).wait_recv()
-    acc_in = [jnp.zeros((train_in.shape[0], HALF_COLS), F32) for _ in range(2)]
-    for q in range(2):
-        for c in range(n):
-            hi, lo = split(r_all[q, c])
-            x = train_in[:, c * rows:(c + 1) * rows]
-            acc_in[q] = acc_in[q] + mm(x, hi, NT) + mm(x, lo, NT)
-    for q in range(2):
-        proj[2 + q] = acc_in[q]
-    swap = remote(proj, proj_theirs, x_sem.at[2], x_sem.at[3], partner)
+        proj[2 + q] = jnp.where(p == q, acc_in[0], acc_in[1])
+    swap = remote(proj, proj_theirs, t_sem.at[0], t_sem.at[1], partner)
     swap.start()
     swap.wait()
 
@@ -477,25 +590,20 @@
         out = src_recv[k] if m == 0 else out + src_recv[k]
     totals[...] = out
 
-    for k in range(1, n):
-        scatter(k).wait_send()
-    for q, k, target in others:
-        right_copy(q, k, target, p, d).wait_send()
-
-    @pl.when(holds)
-    def _():
-        for q, k, target in others:
-            left_copy(q, k, target, p, lax.rem(d, per_core)).wait_send()
-
-    @pl.when(jnp.logical_not(holds))
-    def _():
-        handover.wait_send()
-
-
-def score(n, basis_in, right, left, basis_out, train_out, train_in, member, lens, owner):
+    for k in range(zs):
+        pass_over(k).wait_send()
+        over(k, x).wait_send()
+        cross(k, p).wait_send()
+        corner(k, True).wait_send()
+    for k in range(1, zs):
+        pass_along(k - 1, up[k]).wait_send()
+        along(k, r_all.at[p, d]).wait_send()
+
+
+def score(n, basis_in, right, l_all, train_out, train_in, member, lens, owner):
     rows = basis_in.shape[0] // n
     toks = train_in.shape[0]
-    out_rows = basis_out.shape[0]
+    zs = n // 2
     dma = pltpu.SemaphoreType.DMA
     vm = pltpu.VMEM
     return pl.pallas_call(
@@ -504,21 +612,19 @@
             jax.ShapeDtypeStruct((member.shape[0], 128), F32),
             jax.ShapeDtypeStruct((SOURCES, 128), F32),
         ),
-        in_specs=[pl.BlockSpec(memory_space=pl.ANY)] + [VMEM] * 8,
+        in_specs=[pl.BlockSpec(memory_space=pl.ANY)] + [VMEM] * 7,
         out_specs=(VMEM, VMEM),
         scratch_shapes=[
             vm((n, rows, basis_in.shape[1]), BF16),
-            vm((n, HALF_COLS, rows), F32), vm((n, HALF_COLS, rows), F32),
+            vm((n, HALF_COLS, rows), F32),
+            vm((zs, HALF_COLS, rows), F32), vm((zs, HALF_COLS, rows), F32),
             vm((2, n, HALF_COLS, rows), F32),
-            vm((HALF_COLS, out_rows), F32), vm((HALF_COLS, out_rows), F32),
-            vm((2, n // 2, HALF_COLS, out_rows), F32),
             vm((4, toks, HALF_COLS), F32), vm((4, toks, HALF_COLS), F32),
             vm((SOURCES, 128), F32), vm((n, SOURCES, 128), F32),
-            dma((n,)), dma((n,)), dma((n,)), dma((2, n)), dma((2, n)), dma((2, n)), dma((2, n)),
-            dma((4,)), dma((n,)), dma((n,)),
+            dma((n,)), *[dma((zs,)) for _ in range(12)], dma((2,)), dma((n,)), dma((n,)),
         ],
         compiler_params=params(4),
-    )(basis_in, right, left, basis_out, train_out, train_in, member, lens, owner)
+    )(basis_in, right, l_all, train_out, train_in, member, lens, owner)
 
 
 def body(
@@ -539,11 +645,10 @@
     pairs = query_out.reshape(HALF_Q, 2, QLEN, query_out.shape[1])
     odd = ((jnp.arange(HALF_Q, dtype=jnp.int32) + p) % 2)[:, None, None]
     own_query_out = jnp.where(odd == 0, pairs[:, 0], pairs[:, 1]).reshape(HALF_TOK, -1)
-    out_part = jnp.dot(own_query_out, basis_out, preferred_element_type=F32)
-    q_all, a = gather(n, query_in, out_part)
-    b = rotate(q_all, basis_in, 256)
+    q_all, a_part = gather(n, query_in, own_query_out, basis_out)
+    b, a = rotate(n, q_all, basis_in, a_part, 256)
     left = sketch_left(n, b, sketch_bucket[None], sketch_sign[None], eigval, a)
-    right = right_factors(left, a, eigval, b, 256)
+    right, l_all = right_factors(n, left, a, basis_out, eigval, b, 256)
 
     seqs = lengths.shape[1]
     toks = train_out.shape[0]
@@ -559,7 +664,7 @@
     lens = jnp.pad(seq_len.astype(F32)[:, None], ((0, pad_rows), (0, 0)), constant_values=1.0)
     owner = (source_of_seq[None, :] == jnp.arange(SOURCES, dtype=jnp.int32)[:, None]).astype(F32)
     owner = jnp.pad(owner, ((0, 0), (0, pad_rows)))
-    scores, totals = score(n, basis_in, right, left, basis_out, train_out, train_in, member, lens, owner)
+    scores, totals = score(n, basis_in, right, l_all, train_out, train_in, member, lens, owner)
     return (scores[:seqs, :QUERIES], totals[:, :QUERIES])
 
 

time: 229 us -> 182 us (0.79)
  Pallas kernels: 218 us -> 173 us
  matrix products: 2.86 us -> 0 us
    pallas_call x1, Pallas kernels: 95.7 us -> 52.1 us  [score(): pl.pallas_call(functools.partial(score_kernel, n), out_shape=(jax.ShapeDt...]
    dot_general x1 -> x0, matrix products: 2.86 us -> none  [body(): out_part = jnp.dot(own_query_out, basis_out, preferred_element_type=F32)]
where the time goes in v2:
time: 182 us
  Pallas kernels  173 us (95%)
  local copies, waits for them, and re-layouts  5.59 us (3%)
  other arithmetic  2.2 us (1%)
    pallas_call x1, Pallas kernels, score(): pl.pallas_call(functools.partial(score_kernel, n), out_shape=(jax.ShapeDt...  52.1 us
    pallas_call x1, Pallas kernels, sketch_left(): pl.pallas_call(functools.partial(sketch_kernel, n), grid=(n,), out_shape=...  36.3 us
    pallas_call x1, Pallas kernels, gather(): pl.pallas_call(functools.partial(gather_kernel, zs), out_shape=(jax.Shape...  31 us
    pallas_call x1, Pallas kernels, rotate(): pl.pallas_call(functools.partial(rotate_kernel, n, tiles), grid=(tiles,),...  30.7 us
    pallas_call x1, Pallas kernels, right_factors(): pl.pallas_call(functools.partial(right_kernel, n, tiles), grid=(tiles,),...  23.2 us

profile of v2, /device:TPU:0, one launch (start us, length us, event | category | flops | bytes accessed | tf_op | source)
XLA Modules:
  0.0 181.9 jit_solution(2704694704305179323)
XLA Ops:
  0.6 0.9 fusion.3
  1.5 0.1 broadcast_in_dim.26
  1.6 0.1 broadcast_in_dim.27
  1.7 0.7 bitcast_select_fusion.qout
  2.4 31.0 %shard_map.122 = (bf16[64,7168]{1,0:T(8,128)(2,1)}, f32[64,2048]{1,0:T(8,128)}) custom-call(bf16[16,7168]{1,0:T(8,128)(2,1)} %qin.1, bf16[64,512]{1,0:T(8,128)(2,1)} %bitcast_select_fusion.qout, bf16[512,2048]{1,0:T(8,128)(2,1)} %basis_out.1), custom_call_target="tpu_custom_call" | custom-call | tf_op jit(solution)/shard_map/pallas_call | solution.py:122
  33.5 0.0 copy-start
  33.5 0.0 copy-start.1
  33.5 30.7 %shard_map.123 = (f32[64,1792]{1,0:T(8,128)}, f32[64,2048]{1,0:T(8,128)}) custom-call(bf16[64,7168]{1,0:T(8,128)(2,1)} %get-tuple-element.10.q_all, bf16[7168,1792]{1,0:T(8,128)(2,1)} %basis_in.1, f32[64,2048]{1,0:T(8,128)} %get-tuple-element.11.a_in), custom_call_target="tpu_custom_call" | custom-call | tf_op jit(solution)/shard_map/pallas_call | solution.py:194
  64.2 0.0 copy-done
  64.2 0.6 broadcast_in_dim.29.bucket
  64.8 0.6 broadcast_in_dim.30.sign
  65.4 36.3 %shard_map.124.left = f32[32,2048]{1,0:T(8,128)} custom-call(f32[64,1792]{1,0:T(8,128)} %get-tuple-element.12.b_ref, s32[1,1792]{1,0:T(1,128)} %broadcast_in_dim.29.bucket, s32[1,1792]{1,0:T(1,128)} %broadcast_in_dim.30.sign, bf16[2048,1792]{1,0:T(8,128)(2,1)} %eig.3, f32[64,2048]{1,0:T(8,128)} %get-tuple-element.13.a_ref), custom_call_target="tpu_custom_call" | custom-call | tf_op jit(solution)/shard_map/pallas_call | solution.py:303
  101.7 0.0 copy-start.2
  101.7 0.0 copy-start.3
  101.8 23.2 %shard_map.125 = (f32[32,1792]{1,0:T(8,128)}, f32[2,4,32,512]{3,2,1,0:T(8,128)}) custom-call(f32[32,2048]{1,0:T(8,128)} %shard_map.124.left, f32[64,2048]{1,0:T(8,128)} %get-tuple-element.13.a_ref, bf16[512,2048]{1,0:T(8,128)(2,1)} %basis_out.1, bf16[2048,1792]{1,0:T(8,128)(2,1)} %eig.3, f32[64,1792]{1,0:T(8,128)} %get-tuple-element.12.b_ref), custom_call_target="tpu_custom_call" | custom-call | tf_op jit(solution)/shard_map/pallas_call | solution.py:407
  125.0 0.2 reduce-window.7
  125.2 0.1 fusion
  125.3 0.6 pad_convert_fusion.1.member
  125.9 0.1 copy.15
  126.0 0.6 pad.18.lens
  126.6 0.6 pad_convert_fusion.owner
  127.2 52.1 %shard_map.126 = (f32[8,128]{1,0:T(8,128)}, f32[32,128]{1,0:T(8,128)}) custom-call(bf16[7168,1792]{1,0:T(8,128)(2,1)} %basis_in.1, f32[32,1792]{1,0:T(8,128)} %get-tuple-element.14.right, f32[2,4,32,512]{3,2,1,0:T(8,128)} %get-tuple-element.15.l_all, bf16[128,2048]{1,0:T(8,128)(2,1)} %train_out.1, bf16[128,7168]{1,0:T(8,128)(2,1)} %train_in.1, ...), custom_call_target="tpu_custom_call" | custom-call | tf_op jit(solution)/shard_map/pallas_call | solution.py:609
  179.3 1.4 copy.16
  180.7 1.2 slice.14
  (7 shorter events, 0.0 us)
Async XLA Ops:
  33.5 30.8 %copy-start = (s32[1792]{0:T(1024)S(1)}, s32[1792]{0:T(1024)}, u32[]{:S(2)}) copy-start(s32[1792]{0:T(1024)} %param.18) | copy-start | bytes 21508
  33.5 31.4 %copy-start.1 = (s32[1792]{0:T(1024)S(1)}, s32[1792]{0:T(1024)}, u32[]{:S(2)}) copy-start(s32[1792]{0:T(1024)} %param.19) | copy-start | bytes 21508
  101.7 23.3 %copy-start.2 = (s32[1,4]{1,0:T(1,128)S(1)}, s32[1,4]{1,0:T(1,128)}, u32[]{:S(2)}) copy-start(s32[1,4]{1,0:T(1,128)} %param.20) | copy-start | bytes 52
  101.7 24.8 %copy-start.3 = (s32[4]{0:T(128)S(1)}, s32[4]{0:T(128)}, u32[]{:S(2)}) copy-start(s32[4]{0:T(128)} %param.21) | copy-start | bytes 52

commit v3 on v2

--- a/solution.py
+++ b/solution.py
@@ -73,47 +73,65 @@
     own = pl.ds(pl.multiple_of(z * QLEN, QLEN), QLEN)
     is_sender = x == lax.rem(z + p, 2)
 
-    def along(k):
-        return remote(qin, q_all.at[own], z_send.at[k], z_recv.at[z], {"dp": 2 * lax.rem(z + k, zs) + x})
-
-    def over(j):
-        rows = q_all.at[j * QLEN:(j + 1) * QLEN]
-        return remote(rows, rows, x_send.at[j], x_recv.at[j], across)
+    halves = 2
+    width = qin.shape[1] // halves
+
+    def columns(h):
+        return pl.ds(h * width, width)
+
+    def along(k, h):
+        return remote(
+            qin.at[:, columns(h)], q_all.at[own, columns(h)], z_send.at[h, k], z_recv.at[h, z],
+            {"dp": 2 * lax.rem(z + k, zs) + x},
+        )
+
+    def over(j, h):
+        rows = q_all.at[j * QLEN:(j + 1) * QLEN, columns(h)]
+        return remote(rows, rows, x_send.at[h, j], x_recv.at[h, j], across)
 
     @pl.when(is_sender)
     def _():
-        for k in range(1, zs):
-            along(k).start()
+        for h in range(halves):
+            for k in range(1, zs):
+                along(k, h).start()
         q_all[own, :] = qin[...]
 
+    def forward(j, h, local):
+        in_column = x == lax.rem(j + p, 2)
+
+        @pl.when(jnp.logical_and(in_column, (z == j) if local else (z != j)))
+        def _():
+            if not local:
+                rows = q_all.at[j * QLEN:(j + 1) * QLEN, columns(h)]
+                remote(qin.at[:, columns(h)], rows, z_send.at[h, 0], z_recv.at[h, j], across).wait_recv()
+            over(j, h).start()
+
+    for j in range(zs):
+        for h in range(halves):
+            forward(j, h, True)
     part[...] = mm(qout[...], basis[...], NN)
+    for h in range(halves):
+        for j in range(zs):
+            forward(j, h, False)
+
     for j in range(zs):
         in_column = x == lax.rem(j + p, 2)
 
-        @pl.when(jnp.logical_and(in_column, z != j))
-        def _():
-            rows = q_all.at[j * QLEN:(j + 1) * QLEN]
-            remote(qin, rows, z_send.at[0], z_recv.at[j], across).wait_recv()
-
         @pl.when(in_column)
         def _():
-            over(j).start()
-
-    for j in range(zs):
-        in_column = x == lax.rem(j + p, 2)
-
-        @pl.when(in_column)
-        def _():
-            over(j).wait_send()
+            for h in range(halves):
+                over(j, h).wait_send()
 
         @pl.when(jnp.logical_not(in_column))
         def _():
-            over(j).wait_recv()
+            for h in range(halves):
+                over(j, h).wait_recv()
 
     @pl.when(is_sender)
     def _():
-        for k in range(1, zs):
-            along(k).wait_send()
+        for h in range(halves):
+            for k in range(1, zs):
+                along(k, h).wait_send()
 
 
 def gather(n, query_in, query_out, basis_out):
@@ -127,14 +145,14 @@
         ),
         in_specs=[VMEM] * 3,
         out_specs=(VMEM, VMEM),
-        scratch_shapes=[dma((zs,)), dma((zs,)), dma((zs,)), dma((zs,))],
+        scratch_shapes=[dma((2, zs)) for _ in range(4)],
         compiler_params=params(0),
     )(query_in, query_out, basis_out)
 
 
 def rotate_kernel(
-    n, tiles, q_all, basis, a_in, out, a_out, part, recv, a_part, a_sum, a_recv, send_sem, recv_sem,
-    rs_send, rs_recv, ag_send, ag_recv,
+    n, tiles, q_all, basis, a_in, out, a_out, part, recv, a_part, a_recv, send_sem, recv_sem,
+    rs_send, rs_recv,
 ):
     i = pl.program_id(0)
     d = lax.axis_index("dp")
@@ -149,10 +167,6 @@
             rs_send.at[k], rs_recv.at[k], {"dp": peers[k]},
         )
 
-    def share(k, source):
-        theirs = pl.ds(pl.multiple_of(source * rows, rows), rows)
-        return remote(a_sum.at[own], a_sum.at[theirs], ag_send.at[k], ag_recv.at[k], {"dp": peers[k]})
-
     @pl.when(i == 0)
     def _():
         greet([partner] + [{"dp": peers[k]} for k in range(1, n)])
@@ -163,26 +177,17 @@
     part[i] = mm(q_all[...], basis[...], NN)
     remote(part.at[i], recv.at[i], send_sem.at[i], recv_sem.at[i], partner).start()
 
-    @pl.when(i == tiles // 2)
-    def _():
-        total = a_part[own, :]
-        for k in range(1, n):
-            scatter(k).wait_recv()
-            total = total + a_recv[k]
-        a_sum[own, :] = total
-        for k in range(1, n):
-            share(k, d).start()
-
     @pl.when(i == tiles - 1)
     def _():
         width = part.shape[2]
         for j in range(tiles):
             remote(part.at[j], recv.at[j], send_sem.at[j], recv_sem.at[j], partner).wait()
             out[:, j * width:(j + 1) * width] = part[j] + recv[j]
+        total = a_part[own, :]
         for k in range(1, n):
-            share(k, lax.rem(d + n - k, n)).wait()
-            scatter(k).wait_send()
-        a_out[...] = a_sum[...]
+            scatter(k).wait()
+            total = total + a_recv[k]
+        a_out[...] = total
 
 
 def rotate(n, q_all, basis_in, a_part, width):
@@ -196,7 +201,7 @@
         grid=(tiles,),
         out_shape=(
             jax.ShapeDtypeStruct((rows, cols), F32),
-            jax.ShapeDtypeStruct(a_part.shape, F32),
+            jax.ShapeDtypeStruct((a_part.shape[0] // n, a_part.shape[1]), F32),
         ),
         in_specs=[
             pl.BlockSpec((rows, depth), fixed),
@@ -206,25 +211,37 @@
         out_specs=(pl.BlockSpec((rows, cols), fixed), VMEM),
         scratch_shapes=[
             pltpu.VMEM((tiles, rows, width), F32), pltpu.VMEM((tiles, rows, width), F32),
-            pltpu.VMEM(a_part.shape, F32), pltpu.VMEM(a_part.shape, F32),
+            pltpu.VMEM(a_part.shape, F32),
             pltpu.VMEM((n, a_part.shape[0] // n, a_part.shape[1]), F32),
-            dma((tiles,)), dma((tiles,)), dma((n,)), dma((n,)), dma((n,)), dma((n,)),
+            dma((tiles,)), dma((tiles,)), dma((n,)), dma((n,)),
         ],
         compiler_params=params(1),
     )(q_all, basis_in, a_part)
 
 
 def sketch_kernel(
-    n, b_ref, bucket, sign, eig, a_ref, left, bs_hi, bs_lo, part, recv, whole, gram_mine, gram_theirs,
-    rs_send, rs_recv, ag_send, ag_recv, g_sem,
+    n, b_ref, bucket, sign, eig, a_own, left, a_out, bs_hi, bs_lo, prods, a_sum, part, recv, whole,
+    gram_mine, gram_theirs, a_send, a_recv, rs_send, rs_recv, ag_send, ag_recv, g_sem,
 ):
     i = pl.program_id(0)
     d = lax.axis_index("dp")
     partner = {"tensor": 1 - lax.axis_index("tensor")}
 
+    a_rows = a_own.shape[0]
+    own = pl.ds(pl.multiple_of(d * a_rows, a_rows), a_rows)
+
+    def a_copy(k, source):
+        theirs = pl.ds(pl.multiple_of(source * a_rows, a_rows), a_rows)
+        return remote(
+            a_sum.at[own], a_sum.at[theirs], a_send.at[k], a_recv.at[k], {"dp": lax.rem(d + k, n)}
+        )
+
     @pl.when(i == 0)
     def _():
         greet([{"dp": lax.rem(d + k, n)} for k in range(1, n)] + [partner])
+        a_sum[own, :] = a_own[...]
+        for k in range(1, n):
+            a_copy(k, d).start()
         signs = (2 * sign[...] - 1).astype(F32)
         for k in range(RANK):
             table = jnp.where(bucket[...] == k, signs, 0.0)
@@ -233,23 +250,29 @@
             bs_lo[k * HALF_TOK:(k + 1) * HALF_TOK, :] = lo
 
     r_hi, r_lo = split(1.0 / (eig[...].astype(F32) + DAMP))
-    prod = mm(bs_hi[...], r_hi, NT) + mm(bs_lo[...], r_hi, NT) + mm(bs_hi[...], r_lo, NT)
+    prods[i] = mm(bs_hi[...], r_hi, NT) + mm(bs_lo[...], r_hi, NT) + mm(bs_hi[...], r_lo, NT)
     width = eig.shape[0]
-    for k in range(RANK):
-        block = prod[k * HALF_TOK:(k + 1) * HALF_TOK] * a_ref[...]
-        part[i, k * HALF_Q:(k + 1) * HALF_Q, :] = block.reshape(HALF_Q, QLEN, width).sum(axis=1)
 
     def scatter(k):
         to = lax.rem(d + k, n)
         return remote(part.at[to], recv.at[k], rs_send.at[k], rs_recv.at[k], {"dp": to})
 
-    @pl.when(i != d)
-    def _():
-        k = lax.rem(i - d + n, n)
-        remote(part.at[i], recv.at[k], rs_send.at[k], rs_recv.at[k], {"dp": i}).start()
-
     @pl.when(i == n - 1)
     def _():
+        for k in range(1, n):
+            a_copy(k, lax.rem(d + n - k, n)).wait()
+        for c in range(n):
+            columns = a_sum[:, c * width:(c + 1) * width]
+            for k in range(RANK):
+                block = prods[c, k * HALF_TOK:(k + 1) * HALF_TOK, :] * columns
+                part[c, k * HALF_Q:(k + 1) * HALF_Q, :] = block.reshape(HALF_Q, QLEN, width).sum(axis=1)
+
+            @pl.when(d != c)
+            def _():
+                k = lax.rem(c - d + n, n)
+                remote(part.at[c], recv.at[k], rs_send.at[k], rs_recv.at[k], {"dp": c}).start()
+
+        a_out[...] = a_sum[...]
         total = part[d]
         for k in range(1, n):
             scatter(k).wait_recv()
@@ -279,17 +302,18 @@
         copy.wait()
         gram = gram_mine[0:HALF_Q, :] + gram_theirs[0:HALF_Q, :]
         low = [[None] * RANK for _ in range(RANK)]
-        done = []
+        done, inverse = [], []
         for r in range(RANK):
             for k in range(r + 1):
                 value = gram[:, r * RANK + k:r * RANK + k + 1]
                 for m in range(k):
                     value = value - low[r][m] * low[k][m]
-                low[r][k] = jnp.sqrt(value) if k == r else value / low[k][k]
+                low[r][k] = jnp.sqrt(value) if k == r else value * inverse[k]
+            inverse.append(1.0 / low[r][r])
             row = rows[r]
             for k in range(r):
                 row = row - low[r][k] * done[k]
-            row = row / low[r][r]
+            row = row * inverse[r]
             done.append(row)
             left[r * HALF_Q:(r + 1) * HALF_Q, :] = row
 
@@ -303,21 +327,25 @@
     return pl.pallas_call(
         functools.partial(sketch_kernel, n),
         grid=(n,),
-        out_shape=jax.ShapeDtypeStruct((HALF_COLS, own_rows), F32),
+        out_shape=(
+            jax.ShapeDtypeStruct((HALF_COLS, own_rows), F32),
+            jax.ShapeDtypeStruct((toks, own_rows), F32),
+        ),
         in_specs=[
             pl.BlockSpec((toks, cols), fixed),
             pl.BlockSpec((1, cols), fixed),
             pl.BlockSpec((1, cols), fixed),
             pl.BlockSpec((width, cols), lambda i: (i, 0)),
-            pl.BlockSpec((toks, width), lambda i: (0, i)),
+            pl.BlockSpec(a.shape, fixed),
         ],
-        out_specs=pl.BlockSpec((HALF_COLS, own_rows), fixed),
+        out_specs=(pl.BlockSpec((HALF_COLS, own_rows), fixed), pl.BlockSpec((toks, own_rows), fixed)),
         scratch_shapes=[
             pltpu.VMEM((RANK * toks, cols), BF16), pltpu.VMEM((RANK * toks, cols), BF16),
+            pltpu.VMEM((n, RANK * toks, width), F32), pltpu.VMEM((toks, own_rows), F32),
             pltpu.VMEM((n, HALF_COLS, width), F32), pltpu.VMEM((n, HALF_COLS, width), F32),
             pltpu.VMEM((n, HALF_COLS, width), F32),
             pltpu.VMEM((2 * HALF_Q, 128), F32), pltpu.VMEM((2 * HALF_Q, 128), F32),
-            dma((n,)), dma((n,)), dma((n,)), dma((n,)), dma((2,)),
+            *[dma((n,)) for _ in range(6)], dma((2,)),
         ],
         compiler_params=params(2),
     )(b, bucket, sign, eigval, a)
@@ -567,17 +595,17 @@
     swap.wait()
 
     highest = lax.Precision.HIGHEST
-    result = jnp.zeros(scores.shape, F32)
+    result = jnp.zeros((member.shape[0], 128), F32)
     for q in range(2):
         prod = (proj[q] + proj_theirs[q]) * (proj[2 + q] + proj_theirs[2 + q])
         by_col = jnp.dot(member[...], prod, precision=highest, preferred_element_type=F32)
-        col = lax.broadcasted_iota(jnp.int32, (HALF_COLS, scores.shape[1]), 0)
-        query = lax.broadcasted_iota(jnp.int32, (HALF_COLS, scores.shape[1]), 1)
+        col = lax.broadcasted_iota(jnp.int32, (HALF_COLS, 128), 0)
+        query = lax.broadcasted_iota(jnp.int32, (HALF_COLS, 128), 1)
         j = col % HALF_Q
         pick = (query == 2 * j + (j + q) % 2).astype(F32)
         result = result + jnp.dot(by_col, pick, precision=highest, preferred_element_type=F32)
     result = result / lens[...]
-    scores[...] = result
+    scores[...] = result[:scores.shape[0], :QUERIES]
     src[...] = jnp.dot(owner[...], result, precision=highest, preferred_element_type=F32)
     for k in range(1, n):
         remote(src, src_recv.at[k], s_send.at[k], s_recv.at[k], {"dp": peers[k]}).start()
@@ -588,7 +616,7 @@
         k = lax.rem(d - m + n, n)
         src_recv[0] = src[...]
         out = src_recv[k] if m == 0 else out + src_recv[k]
-    totals[...] = out
+    totals[...] = out[:, :QUERIES]
 
     for k in range(zs):
         pass_over(k).wait_send()
@@ -600,7 +628,7 @@
         along(k, r_all.at[p, d]).wait_send()
 
 
-def score(n, basis_in, right, l_all, train_out, train_in, member, lens, owner):
+def score(n, seqs, basis_in, right, l_all, train_out, train_in, member, lens, owner):
     rows = basis_in.shape[0] // n
     toks = train_in.shape[0]
     zs = n // 2
@@ -609,8 +637,8 @@
     return pl.pallas_call(
         functools.partial(score_kernel, n),
         out_shape=(
-            jax.ShapeDtypeStruct((member.shape[0], 128), F32),
-            jax.ShapeDtypeStruct((SOURCES, 128), F32),
+            jax.ShapeDtypeStruct((seqs, QUERIES), F32),
+            jax.ShapeDtypeStruct((SOURCES, QUERIES), F32),
         ),
         in_specs=[pl.BlockSpec(memory_space=pl.ANY)] + [VMEM] * 7,
         out_specs=(VMEM, VMEM),
@@ -646,8 +674,8 @@
     odd = ((jnp.arange(HALF_Q, dtype=jnp.int32) + p) % 2)[:, None, None]
     own_query_out = jnp.where(odd == 0, pairs[:, 0], pairs[:, 1]).reshape(HALF_TOK, -1)
     q_all, a_part = gather(n, query_in, own_query_out, basis_out)
-    b, a = rotate(n, q_all, basis_in, a_part, 256)
-    left = sketch_left(n, b, sketch_bucket[None], sketch_sign[None], eigval, a)
+    b, a_own = rotate(n, q_all, basis_in, a_part, 256)
+    left, a = sketch_left(n, b, sketch_bucket[None], sketch_sign[None], eigval, a_own)
     right, l_all = right_factors(n, left, a, basis_out, eigval, b, 256)
 
     seqs = lengths.shape[1]
@@ -664,8 +692,7 @@
     lens = jnp.pad(seq_len.astype(F32)[:, None], ((0, pad_rows), (0, 0)), constant_values=1.0)
     owner = (source_of_seq[None, :] == jnp.arange(SOURCES, dtype=jnp.int32)[:, None]).astype(F32)
     owner = jnp.pad(owner, ((0, 0), (0, pad_rows)))
-    scores, totals = score(n, basis_in, right, l_all, train_out, train_in, member, lens, owner)
-    return (scores[:seqs, :QUERIES], totals[:, :QUERIES])
+    return score(n, seqs, basis_in, right, l_all, train_out, train_in, member, lens, owner)
 
 
 def sketch_table(bucket_ids, sign_bits):

time: 182 us -> 167 us (0.918)
  Pallas kernels: 173 us -> 158 us
    pallas_call x1, Pallas kernels: 30.7 us -> 21.2 us  [rotate(): pl.pallas_call(functools.partial(rotate_kernel, n, tiles), grid=(tiles,),...]
    pallas_call x1, Pallas kernels: 31 us -> 26.3 us  [gather(): pl.pallas_call(functools.partial(gather_kernel, zs), out_shape=(jax.Shape...]
where the time goes in v3:
time: 167 us; the launch traced here: 166 us
  Pallas kernels  158 us (95%)
  local copies, waits for them, and re-layouts  5.56 us (3%)
  other arithmetic  2.2 us (1%)
    pallas_call x1, Pallas kernels, score(): pl.pallas_call(functools.partial(score_kernel, n), out_shape=(jax.ShapeDt...  50.3 us
    pallas_call x1, Pallas kernels, sketch_left(): pl.pallas_call(functools.partial(sketch_kernel, n), grid=(n,), out_shape=...  35 us
    pallas_call x1, Pallas kernels, gather(): pl.pallas_call(functools.partial(gather_kernel, zs), out_shape=(jax.Shape...  26.3 us
    pallas_call x1, Pallas kernels, right_factors(): pl.pallas_call(functools.partial(right_kernel, n, tiles), grid=(tiles,),...  24.9 us
    pallas_call x1, Pallas kernels, rotate(): pl.pallas_call(functools.partial(rotate_kernel, n, tiles), grid=(tiles,),...  21.2 us

profile of v3, /device:TPU:0, one launch (start us, length us, event | category | flops | bytes accessed | tf_op | source)
XLA Modules:
  0.0 166.2 jit_solution(647222251432911244)
XLA Ops:
  0.6 0.9 fusion.3
  1.5 0.1 broadcast_in_dim.26
  1.6 0.1 broadcast_in_dim.27
  1.7 0.7 bitcast_select_fusion.qout
  2.4 26.3 %shard_map.122 = (bf16[64,7168]{1,0:T(8,128)(2,1)}, f32[64,2048]{1,0:T(8,128)}) custom-call(bf16[16,7168]{1,0:T(8,128)(2,1)} %qin.1, bf16[64,512]{1,0:T(8,128)(2,1)} %bitcast_select_fusion.qout, bf16[512,2048]{1,0:T(8,128)(2,1)} %basis_out.1), custom_call_target="tpu_custom_call" | custom-call | tf_op jit(solution)/shard_map/pallas_call | solution.py:140
  28.7 0.0 copy-start
  28.7 0.0 copy-start.1
  28.7 21.2 %shard_map.123 = (f32[64,1792]{1,0:T(8,128)}, f32[8,2048]{1,0:T(8,128)}) custom-call(bf16[64,7168]{1,0:T(8,128)(2,1)} %get-tuple-element.10.q_all, bf16[7168,1792]{1,0:T(8,128)(2,1)} %basis_in.1, f32[64,2048]{1,0:T(8,128)} %get-tuple-element.11.a_in), custom_call_target="tpu_custom_call" | custom-call | tf_op jit(solution)/shard_map/pallas_call | solution.py:199
  49.9 0.0 copy-done
  49.9 0.6 broadcast_in_dim.29.bucket
  50.5 0.0 copy-done.1
  50.5 0.6 broadcast_in_dim.30.sign
  51.1 35.0 %shard_map.124 = (f32[32,2048]{1,0:T(8,128)}, f32[64,2048]{1,0:T(8,128)}) custom-call(f32[64,1792]{1,0:T(8,128)} %get-tuple-element.12.b_ref, s32[1,1792]{1,0:T(1,128)} %broadcast_in_dim.29.bucket, s32[1,1792]{1,0:T(1,128)} %broadcast_in_dim.30.sign, bf16[2048,1792]{1,0:T(8,128)(2,1)} %eig.3, f32[8,2048]{1,0:T(8,128)} %get-tuple-element.13.a_own), custom_call_target="tpu_custom_call" | custom-call | tf_op jit(solution)/shard_map/pallas_call | solution.py:327
  86.2 24.9 %shard_map.125 = (f32[32,1792]{1,0:T(8,128)}, f32[2,4,32,512]{3,2,1,0:T(8,128)}) custom-call(f32[32,2048]{1,0:T(8,128)} %get-tuple-element.14.left, f32[64,2048]{1,0:T(8,128)} %get-tuple-element.15.a_ref, bf16[512,2048]{1,0:T(8,128)(2,1)} %basis_out.1, bf16[2048,1792]{1,0:T(8,128)(2,1)} %eig.3, f32[64,1792]{1,0:T(8,128)} %get-tuple-element.12.b_ref), custom_call_target="tpu_custom_call" | custom-call | tf_op jit(solution)/shard_map/pallas_call | solution.py:435
  111.1 0.0 copy-done.2
  111.1 0.2 reduce-window.7
  111.3 0.1 fusion
  111.4 0.6 pad_convert_fusion.1.member
  112.0 0.1 copy.15
  112.1 0.6 pad.18.lens
  112.7 0.6 pad_convert_fusion.owner
  113.3 50.3 %shard_map.126 = (f32[4,8]{1,0:T(4,128)}, f32[32,8]{1,0:T(8,128)}) custom-call(bf16[7168,1792]{1,0:T(8,128)(2,1)} %basis_in.1, f32[32,1792]{1,0:T(8,128)} %get-tuple-element.16.right, f32[2,4,32,512]{3,2,1,0:T(8,128)} %get-tuple-element.17.l_all, bf16[128,2048]{1,0:T(8,128)(2,1)} %train_out.1, bf16[128,7168]{1,0:T(8,128)(2,1)} %train_in.1, ...), custom_call_target="tpu_custom_call" | custom-call | tf_op jit(solution)/shard_map/pallas_call | solution.py:637
  163.6 1.4 copy.16
  165.0 1.2 copy.20
  (7 shorter events, 0.0 us)
Async XLA Ops:
  28.7 21.2 %copy-start = (s32[1792]{0:T(1024)S(1)}, s32[1792]{0:T(1024)}, u32[]{:S(2)}) copy-start(s32[1792]{0:T(1024)} %param.18) | copy-start | bytes 21508
  28.7 21.8 %copy-start.1 = (s32[1792]{0:T(1024)S(1)}, s32[1792]{0:T(1024)}, u32[]{:S(2)}) copy-start(s32[1792]{0:T(1024)} %param.19) | copy-start | bytes 21508
  51.1 60.0 %copy-start.2 = (s32[1,4]{1,0:T(1,128)S(1)}, s32[1,4]{1,0:T(1,128)}, u32[]{:S(2)}) copy-start(s32[1,4]{1,0:T(1,128)} %param.20) | copy-start | bytes 52
  51.1 61.5 %copy-start.3 = (s32[4]{0:T(128)S(1)}, s32[4]{0:T(128)}, u32[]{:S(2)}) copy-start(s32[4]{0:T(128)} %param.21) | copy-start | bytes 52
